TPU v7x, 32 devices: a whole 2x2x4 slice. The times are simulated.
32 devices in a mesh: gx: 2 (over core), gy: 4 (over z), gz: 4 (over y, x).
Axes of the slice: x: 2, y: 2, z: 4, core: 2. Of those that a mesh axis runs over, the one named last changes fastest.
Arguments:
- heat_source: float32 [32, 64, 512], P('gx', 'gy', 'gz'), may hold values from -6 to 6
- material: int32 [32, 64, 512], P('gx', 'gy', 'gz'), may hold values from 0 to 2
- conductivity: float32 [3], replicated, may hold values from 0.3 to 3
Outputs:
- temperature: float32 [32, 64, 512], P('gx', 'gy', 'gz')
All inputs are finite; a program needn't handle non-finite values.
Results may differ from a plain program's by a relative error of at most 0.00002.
Values sent between devices are 32-bit elements; how exact they have to be, the bound alone decides.
A program may use at most 192 MiB of HBM per device.

v0:
```python
import jax
import jax.numpy as jnp
from jax import lax
from jax.sharding import PartitionSpec as P

DEGREE = 3
LEVELS = 3
MATERIALS = 3


LOW = 0.3
HIGH = 2.0


def with_halo(block, sides, width):
    for axis, dim in sides:
        count = lax.axis_size(axis)
        forward = [(i, i + 1) for i in range(count - 1)]
        backward = [(target, source) for source, target in forward]
        low = lax.ppermute(
            lax.slice_in_dim(block, block.shape[dim] - width, None, axis=dim), axis, forward
        )
        high = lax.ppermute(lax.slice_in_dim(block, 0, width, axis=dim), axis, backward)
        block = jnp.concatenate([low, block, high], axis=dim)
    return block


def harmonic(left, right):
    return 2.0 * left * right / (left + right)


def neighbours(padded):
    return (
        padded[2:, 1:-1, 1:-1],
        padded[:-2, 1:-1, 1:-1],
        padded[1:-1, 2:, 1:-1],
        padded[1:-1, :-2, 1:-1],
        padded[1:-1, 1:-1, 2:],
        padded[1:-1, 1:-1, :-2],
    )


def spread_field(field):
    return with_halo(field, (("gx", 0), ("gy", 1), ("gz", 2)), 1)


def spread_cond(cond):
    return with_halo(cond, (("gx", 0), ("gy", 1), ("gz", 2)), 1)


def face_set(cond, extend_cond):
    padded = extend_cond(cond)
    faces = tuple(
        (harmonic(cond, jnp.where(other > 0.0, other, cond)) for other in neighbours(padded))
    )
    diag = faces[0] + faces[1] + faces[2] + faces[3] + faces[4] + faces[5]
    return (faces, diag)


def operate(field, faces, diag, scale, extend_field):
    near = neighbours(extend_field(field))
    total = faces[0] * near[0] + faces[1] * near[1] + faces[2] * near[2]
    total = total + faces[3] * near[3] + faces[4] * near[4] + faces[5] * near[5]
    return scale * (diag * field - total)


def smooth(right, start, faces, diag, scale, extend_field):
    theta = 0.5 * (HIGH + LOW)
    delta = 0.5 * (HIGH - LOW)
    sigma = theta / delta
    rho = 1.0 / sigma
    inverse = 1.0 / (scale * diag)
    if start is None:
        resid = right
        step_dir = inverse * resid / theta
        field = step_dir
    else:
        resid = right - operate(start, faces, diag, scale, extend_field)
        step_dir = inverse * resid / theta
        field = start + step_dir
    for turn in range(DEGREE - 1):
        rho_new = 1.0 / (2.0 * sigma - rho)
        resid = right - operate(field, faces, diag, scale, extend_field)
        step_dir = rho_new * rho * step_dir + 2.0 * rho_new / delta * inverse * resid
        field = field + step_dir
        rho = rho_new
    return field


def restrict(field):
    sx, sy, sz = field.shape
    return field.reshape(sx // 2, 2, sy // 2, 2, sz // 2, 2).mean(axis=(1, 3, 5))


def prolong(field):
    return jnp.repeat(jnp.repeat(jnp.repeat(field, 2, 0), 2, 1), 2, 2)


def cycle(right, cond, level, scale, extend_field, extend_cond):
    faces, diag = face_set(cond, extend_cond)
    if level == LEVELS:
        field = smooth(right, None, faces, diag, scale, extend_field)
        return smooth(right, field, faces, diag, scale, extend_field)
    field = smooth(right, None, faces, diag, scale, extend_field)
    resid = right - operate(field, faces, diag, scale, extend_field)
    error = cycle(
        restrict(resid), restrict(cond), level + 1, scale * 0.25, extend_field, extend_cond
    )
    field = field + prolong(error)
    return smooth(right, field, faces, diag, scale, extend_field)


def local(heat_source, material, conductivity):
    cond = jnp.zeros(heat_source.shape, jnp.float32)
    for which in range(MATERIALS):
        cond = cond + jnp.where(material == which, conductivity[which], jnp.float32(0.0))
    faces, diag = face_set(cond, spread_cond)
    field = smooth(heat_source, None, faces, diag, 1.0, spread_field)
    resid = heat_source - operate(field, faces, diag, 1.0, spread_field)
    coarse_right = restrict(resid)
    coarse_cond = restrict(cond)
    error = cycle(coarse_right, coarse_cond, 1, 0.25, spread_field, spread_cond)
    field = field + prolong(error)
    return smooth(heat_source, field, faces, diag, 1.0, spread_field)


def solution(mesh):
    in_specs = (P("gx", "gy", "gz"), P("gx", "gy", "gz"), P())
    out_specs = P("gx", "gy", "gz")
    return jax.shard_map(local, mesh=mesh, in_specs=in_specs, out_specs=out_specs, check_vma=False)
```

profile of v0, /device:TPU:0, one launch (start us, length us, event | category | flops | bytes accessed | tf_op | source)
XLA Modules:
  0.0 588.6 jit_solution(12443636915279324355)
XLA Ops:
  26.7 6.7 %collective-permute-done.4 = f32[18,18,1]{2,1,0:T(8,128)S(1)} collective-permute-done((f32[18,18,1]{2,1,0:T(8,128)S(1)}, f32[18,18,1]{2,1,0:T(8,128)S(1)}, u32[]{:S(2)}, u32[]{:S(2)}) %collective-permute-start.4) | collective-permute-done | bytes 1328 | tf_op jit(solution)/shard_map/ppermute | solution.py:23
  49.5 4.6 collective-permute-start.11
  61.5 9.7 %reshape.47 = f32[8,2,8,2,64,2]{5,4,3,2,1,0:T(8,128)} reshape(f32[16,16,128]{2,1,0:T(8,128)S(1)} %select_add_fusion) | data formatting | bytes 262144 | tf_op jit(solution)/shard_map/reshape | solution.py:92
  85.8 5.9 %collective-permute-start.17 = (f32[18,18,1]{2,1,0:T(8,128)S(1)}, f32[18,18,1]{2,1,0:T(8,128)S(1)}, u32[]{:S(2)}, u32[]{:S(2)}) collective-permute-start(f32[18,18,1]{2,1,0:T(8,128)S(1)} %get-tuple-element.59), channel_id=1, source_target_pairs={{0,1},{1,2},{2,3},{4,5},{5,6},{6,7},{8,9},{9,10},{10,11},{12,13},{... | collective-permute-start | bytes 3896 | tf_op jit(solution)/shard_map/ppermute | solution.py:20
  103.1 4.5 collective-permute-start.27
  114.7 5.6 collective-permute-start.29
  120.5 5.3 collective-permute-start.23
  127.4 9.7 %reshape.48 = f32[8,2,8,2,64,2]{5,4,3,2,1,0:T(8,128)} reshape(f32[16,16,128]{2,1,0:T(8,128)S(1)} %fusion.48) | data formatting | bytes 262144 | tf_op jit(solution)/shard_map/reshape | solution.py:92
  154.7 5.2 collective-permute-start.35
  175.3 5.4 collective-permute-start.41
  191.4 4.5 collective-permute-start.51
  202.9 5.8 collective-permute-start.53
  208.8 4.8 collective-permute-start.47
  232.6 4.6 collective-permute-start.59
  253.4 5.2 collective-permute-start.65
  270.4 4.8 collective-permute-start.71
  276.6 4.7 collective-permute-start.77
  283.2 4.6 collective-permute-done.70
  303.1 5.4 collective-permute-start.83
  323.1 5.4 collective-permute-start.89
  343.6 5.7 collective-permute-start.95
  363.9 5.7 collective-permute-start.101
  384.2 5.7 collective-permute-start.107
  404.8 5.7 collective-permute-start.113
  425.3 5.7 collective-permute-start.119
  445.8 5.7 collective-permute-start.125
  466.7 5.7 collective-permute-start.131
  487.9 5.7 collective-permute-start.137
  509.0 5.8 collective-permute-start.143
  531.2 5.8 collective-permute-start.149
  554.6 5.9 %collective-permute-start.155 = (f32[18,18,1]{2,1,0:T(8,128)S(1)}, f32[18,18,1]{2,1,0:T(8,128)S(1)}, u32[]{:S(2)}, u32[]{:S(2)}) collective-permute-start(f32[18,18,1]{2,1,0:T(8,128)S(1)} %get-tuple-element.53), channel_id=1, source_target_pairs={{0,1},{1,2},{2,3},{4,5},{5,6},{6,7},{8,9},{9,10},{10,11},{12,13},{... | collective-permute-start | bytes 3896 | tf_op jit(solution)/shard_map/ppermute | solution.py:20
  578.1 5.9 %collective-permute-start.161 = (f32[18,18,1]{2,1,0:T(8,128)S(1)}, f32[18,18,1]{2,1,0:T(8,128)S(1)}, u32[]{:S(2)}, u32[]{:S(2)}) collective-permute-start(f32[18,18,1]{2,1,0:T(8,128)S(1)} %get-tuple-element.51), channel_id=1, source_target_pairs={{0,1},{1,2},{2,3},{4,5},{5,6},{6,7},{8,9},{9,10},{10,11},{12,13},{... | collective-permute-start | bytes 3896 | tf_op jit(solution)/shard_map/ppermute | solution.py:20
  (472 shorter events, 404.0 us)
Async XLA Ops:
  23.1 10.2 %collective-permute-start.4 = (f32[18,18,1]{2,1,0:T(8,128)S(1)}, f32[18,18,1]{2,1,0:T(8,128)S(1)}, u32[]{:S(2)}, u32[]{:S(2)}) collective-permute-start(f32[18,18,1]{2,1,0:T(8,128)S(1)} %get-tuple-element.63), channel_id=1, source_target_pairs={{1,0},{2,1},{3,2},{5,4},{6,5},{7,6},{9,8},{10,9},{11,10},{13,12},{... | collective-permute-start | bytes 3896 | tf_op jit(solution)/shard_map/ppermute | solution.py:23
  48.2 8.6 %collective-permute-start.10 = (f32[18,18,1]{2,1,0:T(8,128)S(1)}, f32[18,18,1]{2,1,0:T(8,128)S(1)}, u32[]{:S(2)}, u32[]{:S(2)}) collective-permute-start(f32[18,18,1]{2,1,0:T(8,128)S(1)} %get-tuple-element.60), channel_id=1, source_target_pairs={{1,0},{2,1},{3,2},{5,4},{6,5},{7,6},{9,8},{10,9},{11,10},{13,12},{... | collective-permute-start | bytes 3896 | tf_op jit(solution)/shard_map/ppermute | solution.py:23
  49.5 8.0 %collective-permute-start.11 = (f32[18,18,1]{2,1,0:T(8,128)S(1)}, f32[18,18,1]{2,1,0:T(8,128)S(1)}, u32[]{:S(2)}, u32[]{:S(2)}) collective-permute-start(f32[18,18,1]{2,1,0:T(8,128)S(1)} %get-tuple-element.61), channel_id=1, source_target_pairs={{0,1},{1,2},{2,3},{4,5},{5,6},{6,7},{8,9},{9,10},{10,11},{12,13},{... | collective-permute-start | bytes 3896 | tf_op jit(solution)/shard_map/ppermute | solution.py:20
  58.8 16.5 %collective-permute-start.13 = (f32[1,16,128]{2,1,0:T(8,128)S(1)}, f32[1,16,128]{2,1,0:T(8,128)S(1)}, u32[]{:S(2)}, u32[]{:S(2)}) collective-permute-start(f32[1,16,128]{2,1,0:T(8,128)S(1)} %get-tuple-element.86), channel_id=1, source_target_pairs={{0,16},{1,17},{2,18},{3,19},{4,20},{5,21},{6,22},{7,23},{8,24},{9,... | collective-permute-start | bytes 24584 | tf_op jit(solution)/shard_map/ppermute | solution.py:20
  60.1 15.2 %collective-permute-start.12 = (f32[1,16,128]{2,1,0:T(8,128)S(1)}, f32[1,16,128]{2,1,0:T(8,128)S(1)}, u32[]{:S(2)}, u32[]{:S(2)}) collective-permute-start(f32[1,16,128]{2,1,0:T(8,128)S(1)} %get-tuple-element.87), channel_id=1, source_target_pairs={{16,0},{17,1},{18,2},{19,3},{20,4},{21,5},{22,6},{23,7},{24,8},{25... | collective-permute-start | bytes 24584 | tf_op jit(solution)/shard_map/ppermute | solution.py:23
  84.5 11.6 %collective-permute-start.16 = (f32[18,18,1]{2,1,0:T(8,128)S(1)}, f32[18,18,1]{2,1,0:T(8,128)S(1)}, u32[]{:S(2)}, u32[]{:S(2)}) collective-permute-start(f32[18,18,1]{2,1,0:T(8,128)S(1)} %get-tuple-element.58), channel_id=1, source_target_pairs={{1,0},{2,1},{3,2},{5,4},{6,5},{7,6},{9,8},{10,9},{11,10},{13,12},{... | collective-permute-start | bytes 3896 | tf_op jit(solution)/shard_map/ppermute | solution.py:23
  85.8 10.4 %collective-permute-start.17 = (f32[18,18,1]{2,1,0:T(8,128)S(1)}, f32[18,18,1]{2,1,0:T(8,128)S(1)}, u32[]{:S(2)}, u32[]{:S(2)}) collective-permute-start(f32[18,18,1]{2,1,0:T(8,128)S(1)} %get-tuple-element.59), channel_id=1, source_target_pairs={{0,1},{1,2},{2,3},{4,5},{5,6},{6,7},{8,9},{9,10},{10,11},{12,13},{... | collective-permute-start | bytes 3896 | tf_op jit(solution)/shard_map/ppermute | solution.py:20
  99.4 9.6 %collective-permute-start.21 = (f32[10,1,64]{2,1,0:T(1,128)S(1)}, f32[10,1,64]{2,1,0:T(1,128)S(1)}, u32[]{:S(2)}, u32[]{:S(2)}) collective-permute-start(f32[10,1,64]{2,1,0:T(1,128)S(1)} %get-tuple-element.118), channel_id=1, source_target_pairs={{0,4},{4,8},{8,12},{1,5},{5,9},{9,13},{2,6},{6,10},{10,14},{3,7},{... | collective-permute-start | bytes 7688 | tf_op jit(solution)/shard_map/ppermute | solution.py:20
  113.4 13.6 %collective-permute-start.28 = (f32[18,18,1]{2,1,0:T(8,128)S(1)}, f32[18,18,1]{2,1,0:T(8,128)S(1)}, u32[]{:S(2)}, u32[]{:S(2)}) collective-permute-start(f32[18,18,1]{2,1,0:T(8,128)S(1)} %get-tuple-element.56), channel_id=1, source_target_pairs={{1,0},{2,1},{3,2},{5,4},{6,5},{7,6},{9,8},{10,9},{11,10},{13,12},{... | collective-permute-start | bytes 3896 | tf_op jit(solution)/shard_map/ppermute | solution.py:23
  114.7 12.3 %collective-permute-start.29 = (f32[18,18,1]{2,1,0:T(8,128)S(1)}, f32[18,18,1]{2,1,0:T(8,128)S(1)}, u32[]{:S(2)}, u32[]{:S(2)}) collective-permute-start(f32[18,18,1]{2,1,0:T(8,128)S(1)} %get-tuple-element.57), channel_id=1, source_target_pairs={{0,1},{1,2},{2,3},{4,5},{5,6},{6,7},{8,9},{9,10},{10,11},{12,13},{... | collective-permute-start | bytes 3896 | tf_op jit(solution)/shard_map/ppermute | solution.py:20
  120.5 20.7 %collective-permute-start.23 = (f32[10,10,1]{2,1,0:T(8,128)S(1)}, f32[10,10,1]{2,1,0:T(8,128)S(1)}, u32[]{:S(2)}, u32[]{:S(2)}) collective-permute-start(f32[10,10,1]{2,1,0:T(8,128)S(1)} %get-tuple-element.104), channel_id=1, source_target_pairs={{0,1},{1,2},{2,3},{4,5},{5,6},{6,7},{8,9},{9,10},{10,11},{12,13},{... | collective-permute-start | bytes 1208 | tf_op jit(solution)/shard_map/ppermute | solution.py:20
  125.7 15.4 %collective-permute-start.22 = (f32[10,10,1]{2,1,0:T(8,128)S(1)}, f32[10,10,1]{2,1,0:T(8,128)S(1)}, u32[]{:S(2)}, u32[]{:S(2)}) collective-permute-start(f32[10,10,1]{2,1,0:T(8,128)S(1)} %get-tuple-element.105), channel_id=1, source_target_pairs={{1,0},{2,1},{3,2},{5,4},{6,5},{7,6},{9,8},{10,9},{11,10},{13,12},{... | collective-permute-start | bytes 1208 | tf_op jit(solution)/shard_map/ppermute | solution.py:23
  174.0 11.3 %collective-permute-start.40 = (f32[10,10,1]{2,1,0:T(8,128)S(1)}, f32[10,10,1]{2,1,0:T(8,128)S(1)}, u32[]{:S(2)}, u32[]{:S(2)}) collective-permute-start(f32[10,10,1]{2,1,0:T(8,128)S(1)} %get-tuple-element.100), channel_id=1, source_target_pairs={{1,0},{2,1},{3,2},{5,4},{6,5},{7,6},{9,8},{10,9},{11,10},{13,12},{... | collective-permute-start | bytes 1208 | tf_op jit(solution)/shard_map/ppermute | solution.py:23
  175.3 10.0 %collective-permute-start.41 = (f32[10,10,1]{2,1,0:T(8,128)S(1)}, f32[10,10,1]{2,1,0:T(8,128)S(1)}, u32[]{:S(2)}, u32[]{:S(2)}) collective-permute-start(f32[10,10,1]{2,1,0:T(8,128)S(1)} %get-tuple-element.101), channel_id=1, source_target_pairs={{0,1},{1,2},{2,3},{4,5},{5,6},{6,7},{8,9},{9,10},{10,11},{12,13},{... | collective-permute-start | bytes 1208 | tf_op jit(solution)/shard_map/ppermute | solution.py:20
  188.2 9.1 %collective-permute-start.45 = (f32[6,1,32]{2,1,0:T(1,128)S(1)}, f32[6,1,32]{2,1,0:T(1,128)S(1)}, u32[]{:S(2)}, u32[]{:S(2)}) collective-permute-start(f32[6,1,32]{2,1,0:T(1,128)S(1)} %get-tuple-element.160), channel_id=1, source_target_pairs={{0,4},{4,8},{8,12},{1,5},{5,9},{9,13},{2,6},{6,10},{10,14},{3,7},{... | collective-permute-start | bytes 2312 | tf_op jit(solution)/shard_map/ppermute | solution.py:20
  201.6 13.5 %collective-permute-start.52 = (f32[10,10,1]{2,1,0:T(8,128)S(1)}, f32[10,10,1]{2,1,0:T(8,128)S(1)}, u32[]{:S(2)}, u32[]{:S(2)}) collective-permute-start(f32[10,10,1]{2,1,0:T(8,128)S(1)} %get-tuple-element.98), channel_id=1, source_target_pairs={{1,0},{2,1},{3,2},{5,4},{6,5},{7,6},{9,8},{10,9},{11,10},{13,12},{... | collective-permute-start | bytes 1208 | tf_op jit(solution)/shard_map/ppermute | solution.py:23
  202.9 12.2 %collective-permute-start.53 = (f32[10,10,1]{2,1,0:T(8,128)S(1)}, f32[10,10,1]{2,1,0:T(8,128)S(1)}, u32[]{:S(2)}, u32[]{:S(2)}) collective-permute-start(f32[10,10,1]{2,1,0:T(8,128)S(1)} %get-tuple-element.99), channel_id=1, source_target_pairs={{0,1},{1,2},{2,3},{4,5},{5,6},{6,7},{8,9},{9,10},{10,11},{12,13},{... | collective-permute-start | bytes 1208 | tf_op jit(solution)/shard_map/ppermute | solution.py:20
  227.1 14.3 %collective-permute-start.66 = (f32[1,2,16]{2,1,0:T(2,128)S(1)}, f32[1,2,16]{2,1,0:T(2,128)S(1)}, u32[]{:S(2)}, u32[]{:S(2)}) collective-permute-start(f32[1,2,16]{2,1,0:T(2,128)S(1)} %get-tuple-element.210), channel_id=1, source_target_pairs={{16,0},{17,1},{18,2},{19,3},{20,4},{21,5},{22,6},{23,7},{24,8},{25... | collective-permute-start | bytes 392 | tf_op jit(solution)/shard_map/ppermute | solution.py:23
  243.2 8.9 %collective-permute-start.63 = (f32[6,1,32]{2,1,0:T(1,128)S(1)}, f32[6,1,32]{2,1,0:T(1,128)S(1)}, u32[]{:S(2)}, u32[]{:S(2)}) collective-permute-start(f32[6,1,32]{2,1,0:T(1,128)S(1)} %get-tuple-element.156), channel_id=1, source_target_pairs={{0,4},{4,8},{8,12},{1,5},{5,9},{9,13},{2,6},{6,10},{10,14},{3,7},{... | collective-permute-start | bytes 2312 | tf_op jit(solution)/shard_map/ppermute | solution.py:20
  247.5 15.4 %collective-permute-start.69 = (f32[4,1,16]{2,1,0:T(1,128)S(1)}, f32[4,1,16]{2,1,0:T(1,128)S(1)}, u32[]{:S(2)}, u32[]{:S(2)}) collective-permute-start(f32[4,1,16]{2,1,0:T(1,128)S(1)} %get-tuple-element.198), channel_id=1, source_target_pairs={{0,4},{4,8},{8,12},{1,5},{5,9},{9,13},{2,6},{6,10},{10,14},{3,7},{... | collective-permute-start | bytes 776 | tf_op jit(solution)/shard_map/ppermute | solution.py:20
  252.2 7.8 %collective-permute-start.64 = (f32[6,6,1]{2,1,0:T(8,128)S(1)}, f32[6,6,1]{2,1,0:T(8,128)S(1)}, u32[]{:S(2)}, u32[]{:S(2)}) collective-permute-start(f32[6,6,1]{2,1,0:T(8,128)S(1)} %get-tuple-element.142), channel_id=1, source_target_pairs={{1,0},{2,1},{3,2},{5,4},{6,5},{7,6},{9,8},{10,9},{11,10},{13,12},{... | collective-permute-start | bytes 440 | tf_op jit(solution)/shard_map/ppermute | solution.py:23
  264.6 10.6 %collective-permute-start.75 = (f32[6,1,32]{2,1,0:T(1,128)S(1)}, f32[6,1,32]{2,1,0:T(1,128)S(1)}, u32[]{:S(2)}, u32[]{:S(2)}) collective-permute-start(f32[6,1,32]{2,1,0:T(1,128)S(1)} %get-tuple-element.154), channel_id=1, source_target_pairs={{0,4},{4,8},{8,12},{1,5},{5,9},{9,13},{2,6},{6,10},{10,14},{3,7},{... | collective-permute-start | bytes 2312 | tf_op jit(solution)/shard_map/ppermute | solution.py:20
  270.4 12.8 %collective-permute-start.71 = (f32[4,4,1]{2,1,0:T(4,128)S(1)}, f32[4,4,1]{2,1,0:T(4,128)S(1)}, u32[]{:S(2)}, u32[]{:S(2)}) collective-permute-start(f32[4,4,1]{2,1,0:T(4,128)S(1)} %get-tuple-element.178), channel_id=1, source_target_pairs={{0,1},{1,2},{2,3},{4,5},{5,6},{6,7},{8,9},{9,10},{10,11},{12,13},{... | collective-permute-start | bytes 200 | tf_op jit(solution)/shard_map/ppermute | solution.py:20
  466.7 7.8 %collective-permute-start.131 = (f32[10,10,1]{2,1,0:T(8,128)S(1)}, f32[10,10,1]{2,1,0:T(8,128)S(1)}, u32[]{:S(2)}, u32[]{:S(2)}) collective-permute-start(f32[10,10,1]{2,1,0:T(8,128)S(1)} %get-tuple-element.97), channel_id=1, source_target_pairs={{0,1},{1,2},{2,3},{4,5},{5,6},{6,7},{8,9},{9,10},{10,11},{12,13},{... | collective-permute-start | bytes 1208 | tf_op jit(solution)/shard_map/ppermute | solution.py:20
  487.9 7.8 %collective-permute-start.137 = (f32[10,10,1]{2,1,0:T(8,128)S(1)}, f32[10,10,1]{2,1,0:T(8,128)S(1)}, u32[]{:S(2)}, u32[]{:S(2)}) collective-permute-start(f32[10,10,1]{2,1,0:T(8,128)S(1)} %get-tuple-element.95), channel_id=1, source_target_pairs={{0,1},{1,2},{2,3},{4,5},{5,6},{6,7},{8,9},{9,10},{10,11},{12,13},{... | collective-permute-start | bytes 1208 | tf_op jit(solution)/shard_map/ppermute | solution.py:20
  509.0 7.9 %collective-permute-start.143 = (f32[10,10,1]{2,1,0:T(8,128)S(1)}, f32[10,10,1]{2,1,0:T(8,128)S(1)}, u32[]{:S(2)}, u32[]{:S(2)}) collective-permute-start(f32[10,10,1]{2,1,0:T(8,128)S(1)} %get-tuple-element.93), channel_id=1, source_target_pairs={{0,1},{1,2},{2,3},{4,5},{5,6},{6,7},{8,9},{9,10},{10,11},{12,13},{... | collective-permute-start | bytes 1208 | tf_op jit(solution)/shard_map/ppermute | solution.py:20
  529.9 9.5 %collective-permute-start.148 = (f32[18,18,1]{2,1,0:T(8,128)S(1)}, f32[18,18,1]{2,1,0:T(8,128)S(1)}, u32[]{:S(2)}, u32[]{:S(2)}) collective-permute-start(f32[18,18,1]{2,1,0:T(8,128)S(1)} %get-tuple-element.54), channel_id=1, source_target_pairs={{1,0},{2,1},{3,2},{5,4},{6,5},{7,6},{9,8},{10,9},{11,10},{13,12},{... | collective-permute-start | bytes 3896 | tf_op jit(solution)/shard_map/ppermute | solution.py:23
  531.2 9.4 %collective-permute-start.149 = (f32[18,18,1]{2,1,0:T(8,128)S(1)}, f32[18,18,1]{2,1,0:T(8,128)S(1)}, u32[]{:S(2)}, u32[]{:S(2)}) collective-permute-start(f32[18,18,1]{2,1,0:T(8,128)S(1)} %get-tuple-element.55), channel_id=1, source_target_pairs={{0,1},{1,2},{2,3},{4,5},{5,6},{6,7},{8,9},{9,10},{10,11},{12,13},{... | collective-permute-start | bytes 3896 | tf_op jit(solution)/shard_map/ppermute | solution.py:20
  553.3 9.6 %collective-permute-start.154 = (f32[18,18,1]{2,1,0:T(8,128)S(1)}, f32[18,18,1]{2,1,0:T(8,128)S(1)}, u32[]{:S(2)}, u32[]{:S(2)}) collective-permute-start(f32[18,18,1]{2,1,0:T(8,128)S(1)} %get-tuple-element.52), channel_id=1, source_target_pairs={{1,0},{2,1},{3,2},{5,4},{6,5},{7,6},{9,8},{10,9},{11,10},{13,12},{... | collective-permute-start | bytes 3896 | tf_op jit(solution)/shard_map/ppermute | solution.py:23
  554.6 9.5 %collective-permute-start.155 = (f32[18,18,1]{2,1,0:T(8,128)S(1)}, f32[18,18,1]{2,1,0:T(8,128)S(1)}, u32[]{:S(2)}, u32[]{:S(2)}) collective-permute-start(f32[18,18,1]{2,1,0:T(8,128)S(1)} %get-tuple-element.53), channel_id=1, source_target_pairs={{0,1},{1,2},{2,3},{4,5},{5,6},{6,7},{8,9},{9,10},{10,11},{12,13},{... | collective-permute-start | bytes 3896 | tf_op jit(solution)/shard_map/ppermute | solution.py:20
  576.8 9.6 %collective-permute-start.160 = (f32[18,18,1]{2,1,0:T(8,128)S(1)}, f32[18,18,1]{2,1,0:T(8,128)S(1)}, u32[]{:S(2)}, u32[]{:S(2)}) collective-permute-start(f32[18,18,1]{2,1,0:T(8,128)S(1)} %get-tuple-element.50), channel_id=1, source_target_pairs={{1,0},{2,1},{3,2},{5,4},{6,5},{7,6},{9,8},{10,9},{11,10},{13,12},{... | collective-permute-start | bytes 3896 | tf_op jit(solution)/shard_map/ppermute | solution.py:23
  578.1 9.5 %collective-permute-start.161 = (f32[18,18,1]{2,1,0:T(8,128)S(1)}, f32[18,18,1]{2,1,0:T(8,128)S(1)}, u32[]{:S(2)}, u32[]{:S(2)}) collective-permute-start(f32[18,18,1]{2,1,0:T(8,128)S(1)} %get-tuple-element.51), channel_id=1, source_target_pairs={{0,1},{1,2},{2,3},{4,5},{5,6},{6,7},{8,9},{9,10},{10,11},{12,13},{... | collective-permute-start | bytes 3896 | tf_op jit(solution)/shard_map/ppermute | solution.py:20
  (131 other events, 661.5 us)
where the time goes:
time: 596 us; the launch traced here: 589 us
  starting transfers between devices  362 us (61%)
  waiting for transfers between devices  177 us (30%)
  local copies, waits for them, and re-layouts  27 us (5%)
  other arithmetic  19.6 us (3%)
    ppermute x81, starting transfers between devices, with_halo(): lax.ppermute(lax.slice_in_dim(block, block.shape[dim] - width, None, axis...  257 us
    ppermute x81, waiting for transfers between devices, with_halo(): lax.ppermute(lax.slice_in_dim(block, 0, width, axis=dim), axis, backward)  152 us
    ppermute x81, starting transfers between devices, with_halo(): lax.ppermute(lax.slice_in_dim(block, 0, width, axis=dim), axis, backward)  105 us
    ppermute x81, waiting for transfers between devices, with_halo(): lax.ppermute(lax.slice_in_dim(block, block.shape[dim] - width, None, axis...  25.2 us
    reshape x4, local copies, waits for them, and re-layouts, restrict(): field.reshape(sx // 2, 2, sy // 2, 2, sz // 2, 2).mean(axis=(1, 3, 5))  20.6 us
  transfers between devices with their start and end apart: 162, of which 81 were waited for; matrix products, arithmetic and copies ran while one was open for 6% of the time, Pallas kernels for 0%

commit v1 on v0

v1 whole, which is shorter than its diff:
```python
import functools

import jax
import jax.numpy as jnp
from jax import lax
from jax.experimental import pallas as pl
from jax.experimental.pallas import tpu as pltpu
from jax.sharding import PartitionSpec as P

DEGREE = 3
LEVELS = 3
MATERIALS = 3

LOW = 0.3
HIGH = 2.0
THETA = 0.5 * (HIGH + LOW)
DELTA = 0.5 * (HIGH - LOW)
SIGMA = THETA / DELTA

HX = 6
HY = 8
HZ = 8
MESH = pl.DeviceIdType.MESH
F32 = jnp.float32


def chebyshev():
    rho = 1.0 / SIGMA
    pairs = []
    for _ in range(DEGREE - 1):
        new = 1.0 / (2.0 * SIGMA - rho)
        pairs.append((new * rho, 2.0 * new / DELTA))
        rho = new
    return pairs


def up(v, axis):
    return pltpu.roll(v, v.shape[axis] - 1, axis)


def down(v, axis):
    return pltpu.roll(v, 1, axis)


def harmonic(a, b):
    return jnp.where((a > 0.0) & (b > 0.0), 2.0 * a * b / (a + b), 0.0)


def build(cond, n, faces_x, faces_y, faces_z, edge, inverse, scale, ring=False):
    shape = cond.shape[1:]
    row = lax.broadcasted_iota(jnp.int32, shape, 0)
    lane = lax.broadcasted_iota(jnp.int32, shape, 1)

    def plane(i, k, k_low, k_high, fx_low):
        ky_high = jnp.where(row == shape[0] - 1, 0.0, up(k, 0))
        ky_low = jnp.where(row == 0, 0.0, down(k, 0))
        kz_high, kz_low = up(k, 1), down(k, 1)
        if not ring:
            kz_high = jnp.where(lane == shape[1] - 1, 0.0, kz_high)
            kz_low = jnp.where(lane == 0, 0.0, kz_low)
        fx, fy, fz = harmonic(k, k_high), harmonic(k, ky_high), harmonic(k, kz_high)
        missing = jnp.zeros(shape, F32)
        for other in (k_low, k_high, ky_low, ky_high, kz_low, kz_high):
            missing = missing + jnp.where(other > 0.0, 0.0, k)
        diag = fx + fx_low + fy + down(fy, 0) + fz + down(fz, 1) + missing
        faces_x[i] = fx
        faces_y[i] = fy
        faces_z[i] = fz
        edge[i] = missing
        inverse[i] = jnp.where(k > 0.0, 1.0 / (scale * diag), 0.0)
        return fx

    def body(i, carry):
        k, k_low, fx_low = carry
        k_high = cond[i + 1]
        fx = plane(i, k, k_low, k_high, fx_low)
        return k_high, k, fx

    zero = jnp.zeros(shape, F32)
    k, k_low, fx_low = lax.fori_loop(0, n - 1, body, (cond[0], zero, zero))
    plane(n - 1, k, k_low, zero, fx_low)


def first(n, right, inverse, field, step):
    def body(i, _):
        value = inverse[i] * right[i] * (1.0 / THETA)
        field[i] = value
        step[i] = value
        return 0

    lax.fori_loop(0, n, body, 0)


def residuals(lo, hi, right, field, coefs, scale, use):
    faces_x, faces_y, faces_z, edge = coefs[:4]

    def body(i, carry):
        x, flux_low = carry
        x_high = field[i + 1]
        flux = faces_x[i] * (x_high - x)
        flux_y = faces_y[i] * (up(x, 0) - x)
        flux_z = faces_z[i] * (up(x, 1) - x)
        total = (flux - flux_low) + (flux_y - down(flux_y, 0)) + (flux_z - down(flux_z, 1))
        total = total - edge[i] * x
        use(i, x, right[i] + scale * total)
        return x_high, flux

    x = field[lo]
    low = faces_x[lo - 1] * (x - field[lo - 1]) if lo > 0 else jnp.zeros(x.shape, F32)
    lax.fori_loop(lo, hi, body, (x, low), unroll=2)


def sweep(lo, hi, right, field, step, coefs, scale, keep, gain):
    inverse = coefs[4]

    def use(i, x, resid):
        d = gain * (inverse[i] * resid)
        if keep is not None:
            d = d + keep * step[i]
        step[i] = d
        field[i] = x + d

    residuals(lo, hi, right, field, coefs, scale, use)


def pairs_rows(out_rows, in_rows):
    r = lax.broadcasted_iota(jnp.int32, (out_rows, in_rows), 0)
    c = lax.broadcasted_iota(jnp.int32, (out_rows, in_rows), 1)
    return jnp.where((c == 2 * r) | (c == 2 * r + 1), 1.0, 0.0).astype(F32)


def pairs_lanes(in_lanes, out_lanes, shift=0):
    r = lax.broadcasted_iota(jnp.int32, (in_lanes, out_lanes), 0)
    c = lax.broadcasted_iota(jnp.int32, (in_lanes, out_lanes), 1) - shift
    return jnp.where((r == 2 * c) | (r == 2 * c + 1), 1.0, 0.0).astype(F32)


def dot(a, b):
    return jnp.dot(a, b, precision=lax.Precision.HIGHEST, preferred_element_type=F32)


def full_smooth(n, right, field, step, coefs, scale, zero_start):
    if zero_start:
        first(n, right, coefs[4], field, step)
    else:
        sweep(0, n, right, field, step, coefs, scale, None, 1.0 / THETA)
    for keep, gain in chebyshev():
        sweep(0, n, right, field, step, coefs, scale, keep, gain)


def coarse_cycle(levels, level):
    n, cond, right, field, step, coefs, temp, scale = levels[level]
    build(cond, n, *coefs, scale)
    field[n] = jnp.zeros(field.shape[1:], F32)
    full_smooth(n, right, field, step, coefs, scale, True)
    if level == len(levels) - 1:
        full_smooth(n, right, field, step, coefs, scale, False)
        return
    half, below, below_right, below_field = n // 2, *levels[level + 1][1:4]
    rows, lanes = field.shape[1:]
    out_rows, out_lanes = below_field.shape[1:]

    def keep_resid(i, x, resid):
        temp[i] = resid

    residuals(0, n, right, field, coefs, scale, keep_resid)
    merge = pairs_rows(half * out_rows, half * rows)
    squeeze = pairs_lanes(lanes, out_lanes)
    for source, target in ((temp, below_right), (cond, below)):
        both = source[...].reshape(half, 2, rows, lanes)
        both = (both[:, 0] + both[:, 1]).reshape(half * rows, lanes)
        target[...] = (dot(dot(merge, both), squeeze) * 0.125).reshape(half, out_rows, out_lanes)
    coarse_cycle(levels, level + 1)
    error = below_field[pl.ds(0, half)].reshape(half * out_rows, out_lanes)
    split = lax.broadcasted_iota(jnp.int32, (half * rows, half * out_rows), 0) // 2
    split = jnp.where(
        split == lax.broadcasted_iota(jnp.int32, (half * rows, half * out_rows), 1), 1.0, 0.0
    )
    spread = lax.broadcasted_iota(jnp.int32, (out_lanes, lanes), 1) // 2
    spread = jnp.where(
        spread == lax.broadcasted_iota(jnp.int32, (out_lanes, lanes), 0), 1.0, 0.0
    )
    error = dot(dot(split, error), spread).reshape(half, rows, lanes)
    for i in range(half):
        field[2 * i] = field[2 * i] + error[i]
        field[2 * i + 1] = field[2 * i + 1] + error[i]
    full_smooth(n, right, field, step, coefs, scale, False)


def halo_kernel(sizes, heat, material, table, ext, pack, got, sems_out, sems_in):
    nx, ny, nz = sizes
    ix, iy, iz = lax.axis_index("gx"), lax.axis_index("gy"), lax.axis_index("gz")
    bx, by, bz = heat.shape
    ext[...] = jnp.zeros(ext.shape, F32)
    got[...] = jnp.zeros(got.shape, F32)
    own = (pl.ds(HX, bx), pl.ds(HY, by), pl.ds(0, bz))
    ext[(0, *own)] = heat[...]
    cond = jnp.zeros(heat.shape, F32)
    for which in range(MATERIALS):
        cond = cond + jnp.where(material[...] == which, table[which], 0.0)
    ext[(1, *own)] = cond

    sides = []
    for axis, at, count in (("gx", ix, nx), ("gy", iy, ny), ("gz", iz, nz)):
        sides.append((axis, at > 0, at - 1))
        sides.append((axis, at < count - 1, at + 1))

    barrier = pltpu.get_barrier_semaphore()
    for axis, there, other in sides:
        @pl.when(there)
        def _():
            pl.semaphore_signal(barrier, inc=1, device_id={axis: other}, device_id_type=MESH)
    pl.semaphore_wait(barrier, sum(jnp.where(there, 1, 0) for _, there, _ in sides))

    def exchange(which, low_source, low_target, high_source, high_target):
        copies = []
        for turn, (source, target) in enumerate(
            ((low_source, low_target), (high_source, high_target))
        ):
            axis, there, other = sides[which + turn]
            copy = pltpu.make_async_remote_copy(
                src_ref=source,
                dst_ref=target,
                send_sem=sems_out.at[which + turn],
                recv_sem=sems_in.at[which + turn],
                device_id={axis: other},
                device_id_type=MESH,
            )
            copies.append((there, copy))
            pl.when(there)(copy.start)
        pl.when(copies[0][0])(copies[1][1].wait_recv)
        pl.when(copies[1][0])(copies[0][1].wait_recv)
        pl.when(copies[0][0])(copies[0][1].wait_send)
        pl.when(copies[1][0])(copies[1][1].wait_send)

    def rows(start):
        return ext.at[:, pl.ds(HX, bx), pl.ds(start, HY), pl.ds(0, bz)]

    exchange(2, rows(HY), rows(HY + by), rows(by), rows(0))

    lane = lax.broadcasted_iota(jnp.int32, (ext.shape[2], bz), 1)
    for part in range(2):
        low = jnp.zeros((ext.shape[2], bz), F32)
        high = low
        for x in range(bx):
            v = ext[part, HX + x, :, pl.ds(0, bz)]
            mine = (lane >= HZ * x) & (lane < HZ * (x + 1))
            low = jnp.where(mine, pltpu.roll(v, (HZ * x) % bz, 1), low)
            high = jnp.where(mine, pltpu.roll(v, HZ * (x + 1) % bz, 1), high)
        pack[0, part] = low
        pack[1, part] = high
    exchange(4, pack.at[0], got.at[1], pack.at[1], got.at[0])
    for part in range(2):
        left, right = got[0, part], got[1, part]
        for x in range(bx):
            v = jnp.where(lane < HZ, pltpu.roll(right, (bz - HZ * x) % bz, 1), 0.0)
            v = jnp.where(lane >= bz - HZ, pltpu.roll(left, (2 * bz - HZ * (x + 1)) % bz, 1), v)
            ext[part, HX + x, :, pl.ds(bz, bz)] = v

    def planes(start):
        return ext.at[:, pl.ds(start, HX)]

    exchange(0, planes(HX), planes(HX + bx), planes(bx), planes(0))


def pre_kernel(ext, field, packed, fx, fy, fz, edge, inverse, step, temp):
    n = ext.shape[1]
    bx, by, bz = n - 2 * HX, ext.shape[2] - 2 * HY, ext.shape[3] // 2
    right, cond = ext.at[0], ext.at[1]
    coefs = (fx, fy, fz, edge, inverse)
    build(cond, n, *coefs, 1.0, True)
    first(n, right, inverse, field, step)
    for turn, (keep, gain) in enumerate(chebyshev()):
        sweep(2 + turn, n - 2 - turn, right, field, step, coefs, 1.0, keep, gain)

    def keep_resid(i, x, resid):
        temp[i - HX] = resid[HY:HY + by, :bz]

    residuals(HX, HX + bx, right, field, coefs, 1.0, keep_resid)
    merge = pairs_rows(bx // 2 * by // 2, bx // 2 * by)
    result = jnp.zeros((bx // 2 * by // 2, bz), F32)
    for shift, source in (
        (0, temp[...]),
        (bz // 2, cond[pl.ds(HX, bx), pl.ds(HY, by), pl.ds(0, bz)]),
    ):
        both = source.reshape(bx // 2, 2, by, bz)
        both = (both[:, 0] + both[:, 1]).reshape(bx // 2 * by, bz)
        squeeze = pairs_lanes(bz, bz, shift)
        if shift == 0:
            lane = lax.broadcasted_iota(jnp.int32, (bz, bz), 1)
            squeeze = jnp.where(lane < bz // 2, squeeze, 0.0)
        result = result + dot(dot(merge, both), squeeze)
    packed[...] = (result * 0.125).reshape(bx // 2, by // 2, bz)


def gather_kernel(sizes, block, full, sems_out, sems_in):
    nx, ny, nz = sizes
    ix, iy, iz = lax.axis_index("gx"), lax.axis_index("gy"), lax.axis_index("gz")
    partners = []
    for axis, at, count in (("gy", iy, ny), ("gz", iz, nz), ("gx", ix, nx)):
        partners.append([(axis, lax.rem(at + off, count)) for off in range(1, count)])
    full[ix, iz, iy] = block[...]
    barrier = pltpu.get_barrier_semaphore()
    total = 0
    for group in partners:
        for axis, other in group:
            pl.semaphore_signal(barrier, inc=1, device_id={axis: other}, device_id_type=MESH)
            total += 1
    pl.semaphore_wait(barrier, total)
    slot = 0
    sent = []
    for group, source in zip(partners, (full.at[ix, iz, iy], full.at[ix, iz], full.at[ix])):
        copies = []
        for axis, other in group:
            copy = pltpu.make_async_remote_copy(
                src_ref=source,
                dst_ref=source,
                send_sem=sems_out.at[slot],
                recv_sem=sems_in.at[slot],
                device_id={axis: other},
                device_id_type=MESH,
            )
            copy.start()
            copies.append(copy)
            slot += 1
        for copy in copies:
            copy.wait_recv()
        sent += copies
    for copy in sent:
        copy.wait_send()


def post_kernel(sizes, ext, start, full, out, *scratch):
    nx, ny, nz = sizes
    ix, iy, iz = lax.axis_index("gx"), lax.axis_index("gy"), lax.axis_index("gz")
    n = ext.shape[1]
    bx, by, bz = out.shape
    scratch = list(scratch)
    field, step, *coefs = scratch[:7]
    levels, place, scale = [], 7, 0.25
    pad = HX // 2
    for level in range(1, LEVELS + 1):
        cond, right, whole, moves, temp, *five = scratch[place:place + 10]
        place += 10
        planes = cond.shape[0]
        values = whole.at[pl.ds(pad, planes + 1)] if level == 1 else whole
        if level == 1:
            coarse = whole
        levels.append((planes, cond, right, values, moves, tuple(five), temp, scale))
        scale *= 0.25
    _, cond, right = levels[0][:3]

    cx, cy = bx // 2, by // 2
    lane = lax.broadcasted_iota(jnp.int32, (cy, bz), 1)

    def assemble(i, _):
        for px in range(nx):
            for q in range(nz // 2):
                for py in range(ny):
                    one, two = full[px, 2 * q, py, i], full[px, 2 * q + 1, py, i]
                    where = (px * cx + i, pl.ds(py * cy, cy), pl.ds(q * bz, bz))
                    right[where] = jnp.where(lane < bz // 2, one, pltpu.roll(two, bz // 2, 1))
                    cond[where] = jnp.where(lane < bz // 2, pltpu.roll(one, bz // 2, 1), two)
        return 0

    lax.fori_loop(0, cx, assemble, 0)
    zero = jnp.zeros((pad, *coarse.shape[1:]), F32)
    coarse[pl.ds(0, pad)] = zero
    coarse[pl.ds(coarse.shape[0] - pad, pad)] = zero
    coarse_cycle(levels, 0)

    rows, lanes = ext.shape[2:]
    crows, clanes = coarse.shape[1:]
    r = lax.broadcasted_iota(jnp.int32, (rows, crows), 0)
    c = lax.broadcasted_iota(jnp.int32, (rows, crows), 1)
    fine = 2 * (c - cy * iy) + HY
    split = jnp.where((r == fine) | (r == fine + 1), 1.0, 0.0).astype(F32)
    r = lax.broadcasted_iota(jnp.int32, (clanes, lanes), 0)
    c = lax.broadcasted_iota(jnp.int32, (clanes, lanes), 1)
    c = jnp.where(c >= lanes - HZ, c - lanes, c)
    fine = 2 * (r - bz // 2 * iz)
    spread = jnp.where((c == fine) | (c == fine + 1), 1.0, 0.0).astype(F32)

    build(ext.at[1], n, *coefs, 1.0, True)
    window = coarse[pl.ds(cx * ix, n // 2)].reshape(n // 2 * crows, clanes)
    window = dot(window, spread).reshape(n // 2, crows, lanes)
    for i in range(n // 2):
        error = dot(split, window[i])
        field[2 * i] = start[2 * i] + error
        field[2 * i + 1] = start[2 * i + 1] + error
    right = ext.at[0]
    sweep(HX - 2, n - HX + 2, right, field, step, coefs, 1.0, None, 1.0 / THETA)
    for turn, (keep, gain) in enumerate(chebyshev()):
        low = HX - 1 + turn
        sweep(low, n - low, right, field, step, coefs, 1.0, keep, gain)
    for i in range(bx):
        out[i] = field[HX + i, HY:HY + by, :bz]


def local(sizes, heat, material, table):
    nx, ny, nz = sizes
    bx, by, bz = heat.shape
    n, rows, lanes = bx + 2 * HX, by + 2 * HY, 2 * bz
    vmem = pl.BlockSpec(memory_space=pltpu.VMEM)
    smem = pl.BlockSpec(memory_space=pltpu.SMEM)
    limit = 48 * 1024 * 1024
    array = jax.ShapeDtypeStruct
    ext = pl.pallas_call(
        functools.partial(halo_kernel, sizes),
        out_shape=array((2, n, rows, lanes), F32),
        in_specs=[vmem, vmem, smem],
        out_specs=vmem,
        scratch_shapes=[
            pltpu.VMEM((2, 2, rows, bz), F32),
            pltpu.VMEM((2, 2, rows, bz), F32),
            pltpu.SemaphoreType.DMA((6,)),
            pltpu.SemaphoreType.DMA((6,)),
        ],
        compiler_params=pltpu.CompilerParams(
            collective_id=0, has_side_effects=True, vmem_limit_bytes=limit
        ),
    )(heat, material, table)
    fine = pltpu.VMEM((n, rows, lanes), F32)
    start, packed = pl.pallas_call(
        pre_kernel,
        out_shape=[array((n, rows, lanes), F32), array((bx // 2, by // 2, bz), F32)],
        in_specs=[vmem],
        out_specs=[vmem, vmem],
        scratch_shapes=[fine] * 6 + [pltpu.VMEM((bx, by, bz), F32)],
        compiler_params=pltpu.CompilerParams(vmem_limit_bytes=limit),
    )(ext)
    count = nx + ny + nz - 3
    full = pl.pallas_call(
        functools.partial(gather_kernel, sizes),
        out_shape=array((nx, nz, ny, bx // 2, by // 2, bz), F32),
        in_specs=[vmem],
        out_specs=vmem,
        scratch_shapes=[pltpu.SemaphoreType.DMA((count,)), pltpu.SemaphoreType.DMA((count,))],
        compiler_params=pltpu.CompilerParams(
            collective_id=1, has_side_effects=True, vmem_limit_bytes=limit
        ),
    )(packed)
    scratch = [fine] * 7
    for level in range(1, LEVELS + 1):
        shape = (bx * nx >> level, by * ny >> level, max(bz * nz >> level, 128))
        extra = HX if level == 1 else 1
        scratch += [pltpu.VMEM(shape, F32)] * 2
        scratch += [pltpu.VMEM((shape[0] + extra, *shape[1:]), F32)]
        scratch += [pltpu.VMEM(shape, F32)] * 7
    return pl.pallas_call(
        functools.partial(post_kernel, sizes),
        out_shape=array(heat.shape, F32),
        in_specs=[vmem] * 3,
        out_specs=vmem,
        scratch_shapes=scratch,
        compiler_params=pltpu.CompilerParams(vmem_limit_bytes=limit),
    )(ext, start, full)


def with_halo(block, sides):
    for axis, dim in sides:
        count = lax.axis_size(axis)
        forward = [(i, i + 1) for i in range(count - 1)]
        backward = [(target, source) for source, target in forward]
        low = lax.ppermute(
            lax.slice_in_dim(block, block.shape[dim] - 1, None, axis=dim), axis, forward
        )
        high = lax.ppermute(lax.slice_in_dim(block, 0, 1, axis=dim), axis, backward)
        block = jnp.concatenate([low, block, high], axis=dim)
    return block


def neighbours(block):
    padded = with_halo(block, (("gx", 0), ("gy", 1), ("gz", 2)))
    return (
        padded[2:, 1:-1, 1:-1],
        padded[:-2, 1:-1, 1:-1],
        padded[1:-1, 2:, 1:-1],
        padded[1:-1, :-2, 1:-1],
        padded[1:-1, 1:-1, 2:],
        padded[1:-1, 1:-1, :-2],
    )


def large_smooth(right, start, faces, diag, scale):
    inverse = 1.0 / (scale * diag)
    if start is None:
        step = inverse * right / THETA
        field = step
    else:
        step = inverse * large_resid(right, start, faces, diag, scale) / THETA
        field = start + step
    for keep, gain in chebyshev():
        step = keep * step + gain * inverse * large_resid(right, field, faces, diag, scale)
        field = field + step
    return field


def large_resid(right, field, faces, diag, scale):
    total = sum(face * near for face, near in zip(faces, neighbours(field)))
    return right - scale * (diag * field - total)


def restrict(field):
    sx, sy, sz = field.shape
    return field.reshape(sx // 2, 2, sy // 2, 2, sz // 2, 2).mean(axis=(1, 3, 5))


def large_cycle(right, cond, level, scale):
    faces = []
    for other in neighbours(cond):
        other = jnp.where(other > 0.0, other, cond)
        faces.append(2.0 * cond * other / (cond + other))
    diag = sum(faces)
    field = large_smooth(right, None, faces, diag, scale)
    if level < LEVELS:
        resid = large_resid(right, field, faces, diag, scale)
        error = large_cycle(restrict(resid), restrict(cond), level + 1, scale * 0.25)
        for dim in range(3):
            error = jnp.repeat(error, 2, dim)
        field = field + error
    return large_smooth(right, field, faces, diag, scale)


def large(heat, material, table):
    cond = jnp.zeros(heat.shape, F32)
    for which in range(MATERIALS):
        cond = cond + jnp.where(material == which, table[which], 0.0)
    return large_cycle(heat, cond, 0, 1.0)


def solution(mesh):
    sizes = tuple(mesh.shape[axis] for axis in ("gx", "gy", "gz"))

    def run(heat, material, table):
        small = heat.size // 8 <= 1 << 18
        body = functools.partial(local, sizes) if small else large
        spec = P("gx", "gy", "gz")
        return jax.shard_map(
            body, mesh=mesh, in_specs=(spec, spec, P()), out_specs=spec, check_vma=False
        )(heat, material, table)

    return run
```

time: 596 us -> 77.6 us (0.13); the launches traced: 589 us -> 77.4 us
  starting transfers between devices: 362 us -> 0 us
  waiting for transfers between devices: 177 us -> 0 us
  Pallas kernels: 0 us -> 74.9 us
  local copies, waits for them, and re-layouts: 27 us -> 2.46 us
  other arithmetic: 19.6 us -> 0 us
    ppermute x162 -> x0, starting transfers between devices: 362 us -> none  [the longest x81 257 us: with_halo(): lax.ppermute(lax.slice_in_dim(block, block.shape[dim] - width, None, axis...]
    ppermute x162 -> x0, waiting for transfers between devices: 177 us -> none  [the longest x81 152 us: with_halo(): lax.ppermute(lax.slice_in_dim(block, 0, width, axis=dim), axis, backward)]
    pallas_call x0 -> x4, Pallas kernels: none -> 74.9 us  [the longest x1 33 us: local(): pl.pallas_call(functools.partial(post_kernel, sizes), out_shape=array(hea...]
    reshape x10 -> x0, local copies, waits for them, and re-layouts: 21.7 us -> none  [the longest x4 20.6 us: restrict(): field.reshape(sx // 2, 2, sy // 2, 2, sz // 2, 2).mean(axis=(1, 3, 5))]
    reduce_sum x6 -> x0, other arithmetic: 8.54 us -> none  [restrict(): field.reshape(sx // 2, 2, sy // 2, 2, sz // 2, 2).mean(axis=(1, 3, 5))]
    add x24 -> x0, other arithmetic: 8.05 us -> none  [the longest x16 4.53 us: smooth(): field = field + step_dir]
  transfers between devices with their start and end apart: 162 -> 0, of which waited for: 81 -> 0; matrix products, arithmetic and copies ran while one was open for 6% -> 0% of each run, Pallas kernels for 0% -> 0%
where the time goes in v1:
time: 77.6 us; the launch traced here: 77.4 us
  Pallas kernels  74.9 us (97%)
  local copies, waits for them, and re-layouts  2.46 us (3%)
    pallas_call x1, Pallas kernels, local(): pl.pallas_call(functools.partial(post_kernel, sizes), out_shape=array(hea...  33 us
    pallas_call x1, Pallas kernels, local(): pl.pallas_call(functools.partial(gather_kernel, sizes), out_shape=array((...  17.1 us
    pallas_call x1, Pallas kernels, local(): pl.pallas_call(functools.partial(halo_kernel, sizes), out_shape=array((2,...  14 us
    pallas_call x1, Pallas kernels, local(): pl.pallas_call(pre_kernel, out_shape=[array((n, rows, lanes), F32), array...  10.8 us
    unnamed x6, local copies, waits for them, and re-layouts  2.46 us

profile of v1, /device:TPU:0, one launch (start us, length us, event | category | flops | bytes accessed | tf_op | source)
XLA Modules:
  0.0 77.4 jit_solution(268937280292314994)
XLA Ops:
  0.0 0.0 copy-start
  0.0 0.9 %copy-done = f32[16,16,128]{2,1,0:T(8,128)S(1)} copy-done((f32[16,16,128]{2,1,0:T(8,128)S(1)}, f32[16,16,128]{2,1,0:T(8,128)}, u32[]{:S(2)}) %copy-start) | copy-done | bytes 131096
  0.9 0.0 copy-start.1
  0.9 0.9 %copy-done.1 = s32[16,16,128]{2,1,0:T(8,128)S(1)} copy-done((s32[16,16,128]{2,1,0:T(8,128)S(1)}, s32[16,16,128]{2,1,0:T(8,128)}, u32[]{:S(2)}) %copy-start.1) | copy-done | bytes 131096
  1.8 0.0 copy-start.2
  1.8 0.7 copy-done.2
  2.5 14.0 %shard_map.37.ext = f32[2,28,32,256]{3,2,1,0:T(8,128)S(1)} custom-call(f32[16,16,128]{2,1,0:T(8,128)S(1)} %copy-done, s32[16,16,128]{2,1,0:T(8,128)S(1)} %copy-done.1, f32[3]{0:T(128)S(1)} %copy-done.2), custom_call_target="tpu_custom_call" | custom-call | tf_op jit(solution)/shard_map/pallas_call | solution.py:408
  16.5 10.8 %shard_map.38 = (f32[28,32,256]{2,1,0:T(8,128)S(1)}, f32[8,8,128]{2,1,0:T(8,128)S(1)}) custom-call(f32[2,28,32,256]{3,2,1,0:T(8,128)S(1)} %shard_map.37.ext), custom_call_target="tpu_custom_call" | custom-call | tf_op jit(solution)/shard_map/pallas_call | solution.py:424
  27.3 17.1 %shard_map.39.full = f32[2,4,4,8,8,128]{5,4,3,2,1,0:T(8,128)S(1)} custom-call(f32[8,8,128]{2,1,0:T(8,128)S(1)} %get-tuple-element.8.block), custom_call_target="tpu_custom_call" | custom-call | tf_op jit(solution)/shard_map/pallas_call | solution.py:433
  44.4 33.0 %shard_map.40 = f32[16,16,128]{2,1,0:T(8,128)} custom-call(f32[2,28,32,256]{3,2,1,0:T(8,128)S(1)} %shard_map.37.ext, f32[28,32,256]{2,1,0:T(8,128)S(1)} %get-tuple-element.7.start, f32[2,4,4,8,8,128]{5,4,3,2,1,0:T(8,128)S(1)} %shard_map.39.full), custom_call_target="tpu_custom_call" | custom-call | tf_op jit(solution)/shard_map/pallas_call | solution.py:450
Async XLA Ops:
  0.0 0.9 %copy-start = (f32[16,16,128]{2,1,0:T(8,128)S(1)}, f32[16,16,128]{2,1,0:T(8,128)}, u32[]{:S(2)}) copy-start(f32[16,16,128]{2,1,0:T(8,128)} %heat.1) | copy-start | bytes 393220
  0.9 0.9 %copy-start.1 = (s32[16,16,128]{2,1,0:T(8,128)S(1)}, s32[16,16,128]{2,1,0:T(8,128)}, u32[]{:S(2)}) copy-start(s32[16,16,128]{2,1,0:T(8,128)} %material.1) | copy-start | bytes 393220
  1.8 0.7 copy-start.2

commit v2 on v1

--- a/solution.py
+++ b/solution.py
@@ -43,10 +43,11 @@
 
 
 def harmonic(a, b):
-    return jnp.where((a > 0.0) & (b > 0.0), 2.0 * a * b / (a + b), 0.0)
-
-
-def build(cond, n, faces_x, faces_y, faces_z, edge, inverse, scale, ring=False):
+    return 2.0 * a * b / jnp.maximum(a + b, 1e-30)
+
+
+def build(cond, n, right, coefs, field, step, scale, ring=False):
+    faces, over, diagonal = coefs
     shape = cond.shape[1:]
     row = lax.broadcasted_iota(jnp.int32, shape, 0)
     lane = lax.broadcasted_iota(jnp.int32, shape, 1)
@@ -62,12 +63,16 @@
         missing = jnp.zeros(shape, F32)
         for other in (k_low, k_high, ky_low, ky_high, kz_low, kz_high):
             missing = missing + jnp.where(other > 0.0, 0.0, k)
-        diag = fx + fx_low + fy + down(fy, 0) + fz + down(fz, 1) + missing
-        faces_x[i] = fx
-        faces_y[i] = fy
-        faces_z[i] = fz
-        edge[i] = missing
-        inverse[i] = jnp.where(k > 0.0, 1.0 / (scale * diag), 0.0)
+        fy_low, fz_low = down(fy, 0), down(fz, 1)
+        diag = fx + fx_low + fy + fy_low + fz + fz_low + missing
+        inverse = jnp.where(k > 0.0, 1.0 / jnp.maximum(diag, 1e-30), 0.0)
+        for side, face in enumerate((fx, fx_low, fy, fy_low, fz, fz_low)):
+            faces[side, i] = face * inverse
+        value = inverse * (1.0 / scale) * right[i]
+        over[i] = value
+        diagonal[i] = diag * scale
+        field[i] = value * (1.0 / THETA)
+        step[i] = value * (1.0 / THETA)
         return fx
 
     def body(i, carry):
@@ -77,50 +82,42 @@
         return k_high, k, fx
 
     zero = jnp.zeros(shape, F32)
-    k, k_low, fx_low = lax.fori_loop(0, n - 1, body, (cond[0], zero, zero))
+    unroll = True if n <= 8 else 3
+    k, k_low, fx_low = lax.fori_loop(0, n - 1, body, (cond[0], zero, zero), unroll=unroll)
     plane(n - 1, k, k_low, zero, fx_low)
 
 
-def first(n, right, inverse, field, step):
-    def body(i, _):
-        value = inverse[i] * right[i] * (1.0 / THETA)
-        field[i] = value
-        step[i] = value
-        return 0
-
-    lax.fori_loop(0, n, body, 0)
-
-
-def residuals(lo, hi, right, field, coefs, scale, use):
-    faces_x, faces_y, faces_z, edge = coefs[:4]
-
-    def body(i, carry):
-        x, flux_low = carry
-        x_high = field[i + 1]
-        flux = faces_x[i] * (x_high - x)
-        flux_y = faces_y[i] * (up(x, 0) - x)
-        flux_z = faces_z[i] * (up(x, 1) - x)
-        total = (flux - flux_low) + (flux_y - down(flux_y, 0)) + (flux_z - down(flux_z, 1))
-        total = total - edge[i] * x
-        use(i, x, right[i] + scale * total)
-        return x_high, flux
-
-    x = field[lo]
-    low = faces_x[lo - 1] * (x - field[lo - 1]) if lo > 0 else jnp.zeros(x.shape, F32)
-    lax.fori_loop(lo, hi, body, (x, low), unroll=2)
-
-
-def sweep(lo, hi, right, field, step, coefs, scale, keep, gain):
-    inverse = coefs[4]
-
-    def use(i, x, resid):
-        d = gain * (inverse[i] * resid)
+def residuals(lo, hi, field, coefs, use):
+    faces, over = coefs[:2]
+    group = min(hi - lo, 8 if field.shape[1] <= 16 else 4)
+
+    def body(turn, carry):
+        start = lo + turn * group
+        xs = list(carry) + [field[start + j + 1] for j in range(group)]
+        results = []
+        for j in range(group):
+            i, x = start + j, xs[j + 1]
+            along_x = faces[0, i] * xs[j + 2] + faces[1, i] * xs[j]
+            along_y = faces[2, i] * up(x, 0) + faces[3, i] * down(x, 0)
+            along_z = faces[4, i] * up(x, 1) + faces[5, i] * down(x, 1)
+            results.append(((over[i] - x) + along_x) + (along_y + along_z))
+        use(start, xs[1:-1], results)
+        return xs[-2], xs[-1]
+
+    low = field[lo - 1] if lo > 0 else jnp.zeros(field.shape[1:], F32)
+    lax.fori_loop(0, (hi - lo) // group, body, (low, field[lo]))
+
+
+def sweep(lo, hi, field, step, coefs, keep, gain):
+    def use(start, xs, results):
+        moves = [gain * z for z in results]
         if keep is not None:
-            d = d + keep * step[i]
-        step[i] = d
-        field[i] = x + d
-
-    residuals(lo, hi, right, field, coefs, scale, use)
+            moves = [keep * step[start + j] + move for j, move in enumerate(moves)]
+        for j, (x, move) in enumerate(zip(xs, moves)):
+            step[start + j] = move
+            field[start + j] = x + move
+
+    residuals(lo, hi, field, coefs, use)
 
 
 def pairs_rows(out_rows, in_rows):
@@ -139,31 +136,30 @@
     return jnp.dot(a, b, precision=lax.Precision.HIGHEST, preferred_element_type=F32)
 
 
-def full_smooth(n, right, field, step, coefs, scale, zero_start):
-    if zero_start:
-        first(n, right, coefs[4], field, step)
-    else:
-        sweep(0, n, right, field, step, coefs, scale, None, 1.0 / THETA)
+def full_smooth(n, field, step, coefs, zero_start):
+    if not zero_start:
+        sweep(0, n, field, step, coefs, None, 1.0 / THETA)
     for keep, gain in chebyshev():
-        sweep(0, n, right, field, step, coefs, scale, keep, gain)
+        sweep(0, n, field, step, coefs, keep, gain)
 
 
 def coarse_cycle(levels, level):
     n, cond, right, field, step, coefs, temp, scale = levels[level]
-    build(cond, n, *coefs, scale)
+    build(cond, n, right, coefs, field, step, scale)
     field[n] = jnp.zeros(field.shape[1:], F32)
-    full_smooth(n, right, field, step, coefs, scale, True)
+    full_smooth(n, field, step, coefs, True)
     if level == len(levels) - 1:
-        full_smooth(n, right, field, step, coefs, scale, False)
+        full_smooth(n, field, step, coefs, False)
         return
     half, below, below_right, below_field = n // 2, *levels[level + 1][1:4]
     rows, lanes = field.shape[1:]
     out_rows, out_lanes = below_field.shape[1:]
 
-    def keep_resid(i, x, resid):
-        temp[i] = resid
-
-    residuals(0, n, right, field, coefs, scale, keep_resid)
+    def keep_resid(start, xs, results):
+        for j, z in enumerate(results):
+            temp[start + j] = z * coefs[2][start + j]
+
+    residuals(0, n, field, coefs, keep_resid)
     merge = pairs_rows(half * out_rows, half * rows)
     squeeze = pairs_lanes(lanes, out_lanes)
     for source, target in ((temp, below_right), (cond, below)):
@@ -184,7 +180,7 @@
     for i in range(half):
         field[2 * i] = field[2 * i] + error[i]
         field[2 * i + 1] = field[2 * i + 1] + error[i]
-    full_smooth(n, right, field, step, coefs, scale, False)
+    full_smooth(n, field, step, coefs, False)
 
 
 def halo_kernel(sizes, heat, material, table, ext, pack, got, sems_out, sems_in):
@@ -263,20 +259,21 @@
     exchange(0, planes(HX), planes(HX + bx), planes(bx), planes(0))
 
 
-def pre_kernel(ext, field, packed, fx, fy, fz, edge, inverse, step, temp):
+def pre_kernel(ext, faces, over, field, packed, diagonal, step, temp):
     n = ext.shape[1]
     bx, by, bz = n - 2 * HX, ext.shape[2] - 2 * HY, ext.shape[3] // 2
     right, cond = ext.at[0], ext.at[1]
-    coefs = (fx, fy, fz, edge, inverse)
-    build(cond, n, *coefs, 1.0, True)
-    first(n, right, inverse, field, step)
-    for turn, (keep, gain) in enumerate(chebyshev()):
-        sweep(2 + turn, n - 2 - turn, right, field, step, coefs, 1.0, keep, gain)
-
-    def keep_resid(i, x, resid):
-        temp[i - HX] = resid[HY:HY + by, :bz]
-
-    residuals(HX, HX + bx, right, field, coefs, 1.0, keep_resid)
+    coefs = (faces, over, diagonal)
+    build(cond, n, right, coefs, field, step, 1.0, True)
+    for keep, gain in chebyshev():
+        sweep(2, n - 2, field, step, coefs, keep, gain)
+
+    def keep_resid(start, xs, results):
+        for j, z in enumerate(results):
+            i = start + j
+            temp[i - HX] = (z * diagonal[i])[HY:HY + by, :bz]
+
+    residuals(HX, HX + bx, field, coefs, keep_resid)
     merge = pairs_rows(bx // 2 * by // 2, bx // 2 * by)
     result = jnp.zeros((bx // 2 * by // 2, bz), F32)
     for shift, source in (
@@ -330,23 +327,22 @@
         copy.wait_send()
 
 
-def post_kernel(sizes, ext, start, full, out, *scratch):
+def post_kernel(sizes, faces, over, start, full, out, *scratch):
     nx, ny, nz = sizes
     ix, iy, iz = lax.axis_index("gx"), lax.axis_index("gy"), lax.axis_index("gz")
-    n = ext.shape[1]
+    n = start.shape[0]
     bx, by, bz = out.shape
-    scratch = list(scratch)
-    field, step, *coefs = scratch[:7]
-    levels, place, scale = [], 7, 0.25
+    field, step = scratch[:2]
+    levels, place, scale = [], 2, 0.25
     pad = HX // 2
     for level in range(1, LEVELS + 1):
-        cond, right, whole, moves, temp, *five = scratch[place:place + 10]
-        place += 10
+        cond, right, whole, moves, temp, *coefs = scratch[place:place + 8]
+        place += 8
         planes = cond.shape[0]
         values = whole.at[pl.ds(pad, planes + 1)] if level == 1 else whole
         if level == 1:
             coarse = whole
-        levels.append((planes, cond, right, values, moves, tuple(five), temp, scale))
+        levels.append((planes, cond, right, values, moves, tuple(coefs), temp, scale))
         scale *= 0.25
     _, cond, right = levels[0][:3]
 
@@ -369,7 +365,7 @@
     coarse[pl.ds(coarse.shape[0] - pad, pad)] = zero
     coarse_cycle(levels, 0)
 
-    rows, lanes = ext.shape[2:]
+    rows, lanes = start.shape[1:]
     crows, clanes = coarse.shape[1:]
     r = lax.broadcasted_iota(jnp.int32, (rows, crows), 0)
     c = lax.broadcasted_iota(jnp.int32, (rows, crows), 1)
@@ -381,18 +377,18 @@
     fine = 2 * (r - bz // 2 * iz)
     spread = jnp.where((c == fine) | (c == fine + 1), 1.0, 0.0).astype(F32)
 
-    build(ext.at[1], n, *coefs, 1.0, True)
     window = coarse[pl.ds(cx * ix, n // 2)].reshape(n // 2 * crows, clanes)
     window = dot(window, spread).reshape(n // 2, crows, lanes)
     for i in range(n // 2):
         error = dot(split, window[i])
         field[2 * i] = start[2 * i] + error
         field[2 * i + 1] = start[2 * i + 1] + error
-    right = ext.at[0]
-    sweep(HX - 2, n - HX + 2, right, field, step, coefs, 1.0, None, 1.0 / THETA)
+    coefs = (faces, over)
+    low = HX - 2
+    sweep(low, n - low, field, step, coefs, None, 1.0 / THETA)
     for turn, (keep, gain) in enumerate(chebyshev()):
-        low = HX - 1 + turn
-        sweep(low, n - low, right, field, step, coefs, 1.0, keep, gain)
+        low = HX - 2 if turn == 0 else HX
+        sweep(low, n - low, field, step, coefs, keep, gain)
     for i in range(bx):
         out[i] = field[HX + i, HY:HY + by, :bz]
 
@@ -403,7 +399,7 @@
     n, rows, lanes = bx + 2 * HX, by + 2 * HY, 2 * bz
     vmem = pl.BlockSpec(memory_space=pltpu.VMEM)
     smem = pl.BlockSpec(memory_space=pltpu.SMEM)
-    limit = 48 * 1024 * 1024
+    limit = 30 * 1024 * 1024
     array = jax.ShapeDtypeStruct
     ext = pl.pallas_call(
         functools.partial(halo_kernel, sizes),
@@ -421,12 +417,17 @@
         ),
     )(heat, material, table)
     fine = pltpu.VMEM((n, rows, lanes), F32)
-    start, packed = pl.pallas_call(
+    faces, over, start, packed = pl.pallas_call(
         pre_kernel,
-        out_shape=[array((n, rows, lanes), F32), array((bx // 2, by // 2, bz), F32)],
+        out_shape=[
+            array((6, n, rows, lanes), F32),
+            array((n, rows, lanes), F32),
+            array((n, rows, lanes), F32),
+            array((bx // 2, by // 2, bz), F32),
+        ],
         in_specs=[vmem],
-        out_specs=[vmem, vmem],
-        scratch_shapes=[fine] * 6 + [pltpu.VMEM((bx, by, bz), F32)],
+        out_specs=[vmem] * 4,
+        scratch_shapes=[fine] * 2 + [pltpu.VMEM((bx, by, bz), F32)],
         compiler_params=pltpu.CompilerParams(vmem_limit_bytes=limit),
     )(ext)
     count = nx + ny + nz - 3
@@ -440,21 +441,23 @@
             collective_id=1, has_side_effects=True, vmem_limit_bytes=limit
         ),
     )(packed)
-    scratch = [fine] * 7
+    scratch = [fine] * 2
     for level in range(1, LEVELS + 1):
         shape = (bx * nx >> level, by * ny >> level, max(bz * nz >> level, 128))
         extra = HX if level == 1 else 1
         scratch += [pltpu.VMEM(shape, F32)] * 2
         scratch += [pltpu.VMEM((shape[0] + extra, *shape[1:]), F32)]
-        scratch += [pltpu.VMEM(shape, F32)] * 7
+        scratch += [pltpu.VMEM(shape, F32)] * 2
+        scratch += [pltpu.VMEM((6, *shape), F32)]
+        scratch += [pltpu.VMEM(shape, F32)] * 2
     return pl.pallas_call(
         functools.partial(post_kernel, sizes),
         out_shape=array(heat.shape, F32),
-        in_specs=[vmem] * 3,
+        in_specs=[vmem] * 4,
         out_specs=vmem,
         scratch_shapes=scratch,
         compiler_params=pltpu.CompilerParams(vmem_limit_bytes=limit),
-    )(ext, start, full)
+    )(faces, over, start, full)
 
 
 def with_halo(block, sides):

time: 77.6 us -> 53 us (0.68)
  Pallas kernels: 74.9 us -> 50.4 us
    pallas_call x1, Pallas kernels: 33 us -> 14.1 us  [local(): pl.pallas_call(functools.partial(post_kernel, sizes), out_shape=array(hea...]
    pallas_call x1, Pallas kernels: 10.8 us -> 5.17 us  [local(): pl.pallas_call(pre_kernel, out_shape=[array((6, n, rows, lanes), F32), ar...]
where the time goes in v2:
time: 53 us; the launch traced here: 52.9 us
  Pallas kernels  50.4 us (95%)
  local copies, waits for them, and re-layouts  2.46 us (5%)
    pallas_call x1, Pallas kernels, local(): pl.pallas_call(functools.partial(gather_kernel, sizes), out_shape=array((...  17.1 us
    pallas_call x1, Pallas kernels, local(): pl.pallas_call(functools.partial(post_kernel, sizes), out_shape=array(hea...  14.1 us
    pallas_call x1, Pallas kernels, local(): pl.pallas_call(functools.partial(halo_kernel, sizes), out_shape=array((2,...  14 us
    pallas_call x1, Pallas kernels, local(): pl.pallas_call(pre_kernel, out_shape=[array((6, n, rows, lanes), F32), ar...  5.17 us
    unnamed x6, local copies, waits for them, and re-layouts  2.46 us

profile of v2, /device:TPU:0, one launch (start us, length us, event | category | flops | bytes accessed | tf_op | source)
XLA Modules:
  0.0 52.9 jit_solution(10980945673753254904)
XLA Ops:
  0.0 0.0 copy-start
  0.0 0.9 %copy-done = f32[16,16,128]{2,1,0:T(8,128)S(1)} copy-done((f32[16,16,128]{2,1,0:T(8,128)S(1)}, f32[16,16,128]{2,1,0:T(8,128)}, u32[]{:S(2)}) %copy-start) | copy-done | bytes 131096
  0.9 0.0 copy-start.1
  0.9 0.9 %copy-done.1 = s32[16,16,128]{2,1,0:T(8,128)S(1)} copy-done((s32[16,16,128]{2,1,0:T(8,128)S(1)}, s32[16,16,128]{2,1,0:T(8,128)}, u32[]{:S(2)}) %copy-start.1) | copy-done | bytes 131096
  1.8 0.0 copy-start.2
  1.8 0.7 %copy-done.2 = f32[3]{0:T(128)S(1)} copy-done((f32[3]{0:T(128)S(1)}, f32[3]{0:T(128)}, u32[]{:S(2)}) %copy-start.2) | copy-done | bytes 36
  2.5 14.0 %shard_map.37.ext = f32[2,28,32,256]{3,2,1,0:T(8,128)S(1)} custom-call(f32[16,16,128]{2,1,0:T(8,128)S(1)} %copy-done, s32[16,16,128]{2,1,0:T(8,128)S(1)} %copy-done.1, f32[3]{0:T(128)S(1)} %copy-done.2), custom_call_target="tpu_custom_call" | custom-call | tf_op jit(solution)/shard_map/pallas_call | solution.py:404
  16.5 5.2 %shard_map.38 = (f32[6,28,32,256]{3,2,1,0:T(8,128)S(1)}, f32[28,32,256]{2,1,0:T(8,128)S(1)}, f32[28,32,256]{2,1,0:T(8,128)S(1)}, f32[8,8,128]{2,1,0:T(8,128)S(1)}) custom-call(f32[2,28,32,256]{3,2,1,0:T(8,128)S(1)} %shard_map.37.ext), custom_call_target="tpu_custom_call" | custom-call | tf_op jit(solution)/shard_map/pallas_call | solution.py:420
  21.6 17.1 %shard_map.39.full = f32[2,4,4,8,8,128]{5,4,3,2,1,0:T(8,128)S(1)} custom-call(f32[8,8,128]{2,1,0:T(8,128)S(1)} %get-tuple-element.12.block), custom_call_target="tpu_custom_call" | custom-call | tf_op jit(solution)/shard_map/pallas_call | solution.py:434
  38.8 14.1 %shard_map.40 = f32[16,16,128]{2,1,0:T(8,128)} custom-call(f32[6,28,32,256]{3,2,1,0:T(8,128)S(1)} %get-tuple-element.9.faces, f32[28,32,256]{2,1,0:T(8,128)S(1)} %get-tuple-element.10.over, f32[28,32,256]{2,1,0:T(8,128)S(1)} %get-tuple-element.11.start, f32[2,4,4,8,8,128]{5,4,3,2,1,0:T(8,128)S(1)} %shard_map.39.full), custom_call_target="tpu_custom_call" | custom-call | tf_op jit(solution)/shard_map/pallas_call | solution.py:453
Async XLA Ops:
  0.0 0.9 %copy-start = (f32[16,16,128]{2,1,0:T(8,128)S(1)}, f32[16,16,128]{2,1,0:T(8,128)}, u32[]{:S(2)}) copy-start(f32[16,16,128]{2,1,0:T(8,128)} %heat.1) | copy-start | bytes 393220
  0.9 0.9 %copy-start.1 = (s32[16,16,128]{2,1,0:T(8,128)S(1)}, s32[16,16,128]{2,1,0:T(8,128)}, u32[]{:S(2)}) copy-start(s32[16,16,128]{2,1,0:T(8,128)} %material.1) | copy-start | bytes 393220
  1.8 0.7 %copy-start.2 = (f32[3]{0:T(128)S(1)}, f32[3]{0:T(128)}, u32[]{:S(2)}) copy-start(f32[3]{0:T(128)} %table.1) | copy-start | bytes 40

commit v3 on v2

--- a/solution.py
+++ b/solution.py
@@ -183,32 +183,111 @@
     full_smooth(n, field, step, coefs, False)
 
 
-def halo_kernel(sizes, heat, material, table, ext, pack, got, sems_out, sems_in):
+def pack_block(values):
+    bx, by, bz = values.shape
+    rows = bx // 2 * by // 2
+    both = values.reshape(bx // 2, 2, by, bz)
+    both = (both[:, 0] + both[:, 1]).reshape(bx // 2 * by, bz)
+    both = dot(pairs_rows(rows, 2 * rows), both)
+    low = dot(both[:rows // 2], pairs_lanes(bz, bz))
+    high = dot(both[rows // 2:], pairs_lanes(bz, bz, bz // 2))
+    return ((low + high) * 0.125).reshape(bx // 4, by // 2, bz)
+
+
+def partner_groups(sizes, places):
+    groups = []
+    for which in (1, 2, 0):
+        axis, at, count = ("gx", "gy", "gz")[which], places[which], sizes[which]
+        groups.append([(axis, lax.rem(at + off, count)) for off in range(1, count)])
+    return groups
+
+
+def greet(groups):
+    barrier = pltpu.get_barrier_semaphore()
+    for group in groups:
+        for axis, other in group:
+            pl.semaphore_signal(barrier, inc=1, device_id={axis: other}, device_id_type=MESH)
+
+
+def await_greetings(groups):
+    pl.semaphore_wait(pltpu.get_barrier_semaphore(), sum(len(group) for group in groups))
+
+
+def gather_stages(places, groups, full, sems_out, sems_in):
+    ix, iy, iz = places
+    slot = 0
+    stages = []
+    for group, source in zip(groups, (full.at[ix, iz, iy], full.at[ix, iz], full.at[ix])):
+        stage = []
+        for axis, other in group:
+            stage.append(
+                pltpu.make_async_remote_copy(
+                    src_ref=source,
+                    dst_ref=source,
+                    send_sem=sems_out.at[slot],
+                    recv_sem=sems_in.at[slot],
+                    device_id={axis: other},
+                    device_id_type=MESH,
+                )
+            )
+            slot += 1
+        stages.append(stage)
+    return stages
+
+
+def start_stage(stage):
+    for copy in stage:
+        copy.start()
+
+
+def end_stage(stage):
+    for copy in stage:
+        copy.wait_recv()
+
+
+def halo_kernel(
+    sizes, heat, material, table, ext, full,
+    heat_here, material_here, pack, got, sems_out, sems_in, gather_out, gather_in, sems_load,
+):
     nx, ny, nz = sizes
-    ix, iy, iz = lax.axis_index("gx"), lax.axis_index("gy"), lax.axis_index("gz")
+    places = ix, iy, iz = tuple(lax.axis_index(axis) for axis in ("gx", "gy", "gz"))
     bx, by, bz = heat.shape
+    loads = [
+        pltpu.make_async_copy(heat, heat_here, sems_load.at[0]),
+        pltpu.make_async_copy(material, material_here, sems_load.at[1]),
+    ]
+    for load in loads:
+        load.start()
     ext[...] = jnp.zeros(ext.shape, F32)
     got[...] = jnp.zeros(got.shape, F32)
+    groups = partner_groups(sizes, places)
+    greet(groups)
+    for load in loads:
+        load.wait()
     own = (pl.ds(HX, bx), pl.ds(HY, by), pl.ds(0, bz))
-    ext[(0, *own)] = heat[...]
-    cond = jnp.zeros(heat.shape, F32)
+    ext[(0, *own)] = heat_here[...]
+    cond = jnp.zeros((bx, by, bz), F32)
     for which in range(MATERIALS):
-        cond = cond + jnp.where(material[...] == which, table[which], 0.0)
+        cond = cond + jnp.where(material_here[...] == which, table[which], 0.0)
     ext[(1, *own)] = cond
+    lane = lax.broadcasted_iota(jnp.int32, (by, bz), 1)
+    for part in range(2):
+        low = jnp.zeros((by, bz), F32)
+        high = low
+        for x in range(bx):
+            v = ext[part, HX + x, pl.ds(HY, by), pl.ds(0, bz)]
+            mine = (lane >= HZ * x) & (lane < HZ * (x + 1))
+            low = jnp.where(mine, pltpu.roll(v, (HZ * x) % bz, 1), low)
+            high = jnp.where(mine, pltpu.roll(v, HZ * (x + 1) % bz, 1), high)
+        pack[0, part] = low
+        pack[1, part] = high
 
     sides = []
     for axis, at, count in (("gx", ix, nx), ("gy", iy, ny), ("gz", iz, nz)):
         sides.append((axis, at > 0, at - 1))
         sides.append((axis, at < count - 1, at + 1))
 
-    barrier = pltpu.get_barrier_semaphore()
-    for axis, there, other in sides:
-        @pl.when(there)
-        def _():
-            pl.semaphore_signal(barrier, inc=1, device_id={axis: other}, device_id_type=MESH)
-    pl.semaphore_wait(barrier, sum(jnp.where(there, 1, 0) for _, there, _ in sides))
-
-    def exchange(which, low_source, low_target, high_source, high_target):
+    def send(which, slot, low_source, low_target, high_source, high_target):
         copies = []
         for turn, (source, target) in enumerate(
             ((low_source, low_target), (high_source, high_target))
@@ -217,46 +296,62 @@
             copy = pltpu.make_async_remote_copy(
                 src_ref=source,
                 dst_ref=target,
-                send_sem=sems_out.at[which + turn],
-                recv_sem=sems_in.at[which + turn],
+                send_sem=sems_out.at[slot + turn],
+                recv_sem=sems_in.at[slot + turn],
                 device_id={axis: other},
                 device_id_type=MESH,
             )
             copies.append((there, copy))
             pl.when(there)(copy.start)
+        return copies
+
+    def receive(copies):
         pl.when(copies[0][0])(copies[1][1].wait_recv)
         pl.when(copies[1][0])(copies[0][1].wait_recv)
-        pl.when(copies[0][0])(copies[0][1].wait_send)
-        pl.when(copies[1][0])(copies[1][1].wait_send)
 
     def rows(start):
         return ext.at[:, pl.ds(HX, bx), pl.ds(start, HY), pl.ds(0, bz)]
 
-    exchange(2, rows(HY), rows(HY + by), rows(by), rows(0))
-
+    def planes(start):
+        return ext.at[:, pl.ds(start, HX)]
+
+    middle = pl.ds(HY, by)
+    await_greetings(groups)
+    sent = [
+        send(4, 4, pack.at[0], got.at[1, :, middle], pack.at[1], got.at[0, :, middle]),
+        send(2, 2, rows(HY), rows(HY + by), rows(by), rows(0)),
+    ]
+    full[ix, iz, iy] = pack_block(cond)
+    stages = gather_stages(places, groups, full, gather_out, gather_in)
+    start_stage(stages[0])
+    receive(sent[0])
+
+    def edges(start):
+        return got.at[:, :, pl.ds(start, HY)]
+
+    sent.append(send(2, 6, edges(HY), edges(HY + by), edges(by), edges(0)))
+    receive(sent[2])
     lane = lax.broadcasted_iota(jnp.int32, (ext.shape[2], bz), 1)
-    for part in range(2):
-        low = jnp.zeros((ext.shape[2], bz), F32)
-        high = low
-        for x in range(bx):
-            v = ext[part, HX + x, :, pl.ds(0, bz)]
-            mine = (lane >= HZ * x) & (lane < HZ * (x + 1))
-            low = jnp.where(mine, pltpu.roll(v, (HZ * x) % bz, 1), low)
-            high = jnp.where(mine, pltpu.roll(v, HZ * (x + 1) % bz, 1), high)
-        pack[0, part] = low
-        pack[1, part] = high
-    exchange(4, pack.at[0], got.at[1], pack.at[1], got.at[0])
     for part in range(2):
         left, right = got[0, part], got[1, part]
         for x in range(bx):
             v = jnp.where(lane < HZ, pltpu.roll(right, (bz - HZ * x) % bz, 1), 0.0)
             v = jnp.where(lane >= bz - HZ, pltpu.roll(left, (2 * bz - HZ * (x + 1)) % bz, 1), v)
             ext[part, HX + x, :, pl.ds(bz, bz)] = v
-
-    def planes(start):
-        return ext.at[:, pl.ds(start, HX)]
-
-    exchange(0, planes(HX), planes(HX + bx), planes(bx), planes(0))
+    end_stage(stages[0])
+    start_stage(stages[1])
+    receive(sent[1])
+    sent.append(send(0, 0, planes(HX), planes(HX + bx), planes(bx), planes(0)))
+    end_stage(stages[1])
+    start_stage(stages[2])
+    receive(sent[3])
+    end_stage(stages[2])
+    for copies in sent:
+        for there, copy in copies:
+            pl.when(there)(copy.wait_send)
+    for stage in stages:
+        for copy in stage:
+            copy.wait_send()
 
 
 def pre_kernel(ext, faces, over, field, packed, diagonal, step, temp):
@@ -274,60 +369,25 @@
             temp[i - HX] = (z * diagonal[i])[HY:HY + by, :bz]
 
     residuals(HX, HX + bx, field, coefs, keep_resid)
-    merge = pairs_rows(bx // 2 * by // 2, bx // 2 * by)
-    result = jnp.zeros((bx // 2 * by // 2, bz), F32)
-    for shift, source in (
-        (0, temp[...]),
-        (bz // 2, cond[pl.ds(HX, bx), pl.ds(HY, by), pl.ds(0, bz)]),
-    ):
-        both = source.reshape(bx // 2, 2, by, bz)
-        both = (both[:, 0] + both[:, 1]).reshape(bx // 2 * by, bz)
-        squeeze = pairs_lanes(bz, bz, shift)
-        if shift == 0:
-            lane = lax.broadcasted_iota(jnp.int32, (bz, bz), 1)
-            squeeze = jnp.where(lane < bz // 2, squeeze, 0.0)
-        result = result + dot(dot(merge, both), squeeze)
-    packed[...] = (result * 0.125).reshape(bx // 2, by // 2, bz)
+    packed[...] = pack_block(temp[...])
 
 
 def gather_kernel(sizes, block, full, sems_out, sems_in):
-    nx, ny, nz = sizes
-    ix, iy, iz = lax.axis_index("gx"), lax.axis_index("gy"), lax.axis_index("gz")
-    partners = []
-    for axis, at, count in (("gy", iy, ny), ("gz", iz, nz), ("gx", ix, nx)):
-        partners.append([(axis, lax.rem(at + off, count)) for off in range(1, count)])
+    places = ix, iy, iz = tuple(lax.axis_index(axis) for axis in ("gx", "gy", "gz"))
+    groups = partner_groups(sizes, places)
+    greet(groups)
     full[ix, iz, iy] = block[...]
-    barrier = pltpu.get_barrier_semaphore()
-    total = 0
-    for group in partners:
-        for axis, other in group:
-            pl.semaphore_signal(barrier, inc=1, device_id={axis: other}, device_id_type=MESH)
-            total += 1
-    pl.semaphore_wait(barrier, total)
-    slot = 0
-    sent = []
-    for group, source in zip(partners, (full.at[ix, iz, iy], full.at[ix, iz], full.at[ix])):
-        copies = []
-        for axis, other in group:
-            copy = pltpu.make_async_remote_copy(
-                src_ref=source,
-                dst_ref=source,
-                send_sem=sems_out.at[slot],
-                recv_sem=sems_in.at[slot],
-                device_id={axis: other},
-                device_id_type=MESH,
-            )
-            copy.start()
-            copies.append(copy)
-            slot += 1
-        for copy in copies:
-            copy.wait_recv()
-        sent += copies
-    for copy in sent:
-        copy.wait_send()
-
-
-def post_kernel(sizes, faces, over, start, full, out, *scratch):
+    await_greetings(groups)
+    stages = gather_stages(places, groups, full, sems_out, sems_in)
+    for stage in stages:
+        start_stage(stage)
+        end_stage(stage)
+    for stage in stages:
+        for copy in stage:
+            copy.wait_send()
+
+
+def post_kernel(sizes, faces, over, start, full_right, full_cond, out, *scratch):
     nx, ny, nz = sizes
     ix, iy, iz = lax.axis_index("gx"), lax.axis_index("gy"), lax.axis_index("gz")
     n = start.shape[0]
@@ -349,17 +409,17 @@
     cx, cy = bx // 2, by // 2
     lane = lax.broadcasted_iota(jnp.int32, (cy, bz), 1)
 
-    def assemble(i, _):
+    for full, target in ((full_right, right), (full_cond, cond)):
         for px in range(nx):
             for q in range(nz // 2):
                 for py in range(ny):
-                    one, two = full[px, 2 * q, py, i], full[px, 2 * q + 1, py, i]
-                    where = (px * cx + i, pl.ds(py * cy, cy), pl.ds(q * bz, bz))
-                    right[where] = jnp.where(lane < bz // 2, one, pltpu.roll(two, bz // 2, 1))
-                    cond[where] = jnp.where(lane < bz // 2, pltpu.roll(one, bz // 2, 1), two)
-        return 0
-
-    lax.fori_loop(0, cx, assemble, 0)
+                    for i in range(cx // 2):
+                        one, two = full[px, 2 * q, py, i], full[px, 2 * q + 1, py, i]
+                        place = (pl.ds(py * cy, cy), pl.ds(q * bz, bz))
+                        low = jnp.where(lane < bz // 2, one, pltpu.roll(two, bz // 2, 1))
+                        high = jnp.where(lane < bz // 2, pltpu.roll(one, bz // 2, 1), two)
+                        target[(px * cx + i, *place)] = low
+                        target[(px * cx + cx // 2 + i, *place)] = high
     zero = jnp.zeros((pad, *coarse.shape[1:]), F32)
     coarse[pl.ds(0, pad)] = zero
     coarse[pl.ds(coarse.shape[0] - pad, pad)] = zero
@@ -401,16 +461,25 @@
     smem = pl.BlockSpec(memory_space=pltpu.SMEM)
     limit = 30 * 1024 * 1024
     array = jax.ShapeDtypeStruct
-    ext = pl.pallas_call(
+    hbm = pl.BlockSpec(memory_space=pltpu.HBM)
+    count = nx + ny + nz - 3
+    coarse = array((nx, nz, ny, bx // 4, by // 2, bz), F32)
+    dma = pltpu.SemaphoreType.DMA
+    ext, full_cond = pl.pallas_call(
         functools.partial(halo_kernel, sizes),
-        out_shape=array((2, n, rows, lanes), F32),
-        in_specs=[vmem, vmem, smem],
-        out_specs=vmem,
+        out_shape=[array((2, n, rows, lanes), F32), coarse],
+        in_specs=[hbm, hbm, smem],
+        out_specs=[vmem, vmem],
         scratch_shapes=[
+            pltpu.VMEM(heat.shape, F32),
+            pltpu.VMEM(heat.shape, jnp.int32),
+            pltpu.VMEM((2, 2, by, bz), F32),
             pltpu.VMEM((2, 2, rows, bz), F32),
-            pltpu.VMEM((2, 2, rows, bz), F32),
-            pltpu.SemaphoreType.DMA((6,)),
-            pltpu.SemaphoreType.DMA((6,)),
+            dma((8,)),
+            dma((8,)),
+            dma((count,)),
+            dma((count,)),
+            dma((2,)),
         ],
         compiler_params=pltpu.CompilerParams(
             collective_id=0, has_side_effects=True, vmem_limit_bytes=limit
@@ -423,17 +492,16 @@
             array((6, n, rows, lanes), F32),
             array((n, rows, lanes), F32),
             array((n, rows, lanes), F32),
-            array((bx // 2, by // 2, bz), F32),
+            array((bx // 4, by // 2, bz), F32),
         ],
         in_specs=[vmem],
         out_specs=[vmem] * 4,
         scratch_shapes=[fine] * 2 + [pltpu.VMEM((bx, by, bz), F32)],
         compiler_params=pltpu.CompilerParams(vmem_limit_bytes=limit),
     )(ext)
-    count = nx + ny + nz - 3
-    full = pl.pallas_call(
+    full_right = pl.pallas_call(
         functools.partial(gather_kernel, sizes),
-        out_shape=array((nx, nz, ny, bx // 2, by // 2, bz), F32),
+        out_shape=coarse,
         in_specs=[vmem],
         out_specs=vmem,
         scratch_shapes=[pltpu.SemaphoreType.DMA((count,)), pltpu.SemaphoreType.DMA((count,))],
@@ -453,11 +521,11 @@
     return pl.pallas_call(
         functools.partial(post_kernel, sizes),
         out_shape=array(heat.shape, F32),
-        in_specs=[vmem] * 4,
+        in_specs=[vmem] * 5,
         out_specs=vmem,
         scratch_shapes=scratch,
         compiler_params=pltpu.CompilerParams(vmem_limit_bytes=limit),
-    )(faces, over, start, full)
+    )(faces, over, start, full_right, full_cond)
 
 
 def with_halo(block, sides):

time: 53 us -> 50.9 us (0.960)
  Pallas kernels: 50.4 us -> 48.3 us
    pallas_call x2, Pallas kernels: 31.1 us -> 29.4 us  [the longest x1 18.1 us: local(): pl.pallas_call(functools.partial(halo_kernel, sizes), out_shape=[array((2...]
where the time goes in v3:
time: 50.9 us; the launch traced here: 50.8 us
  Pallas kernels  48.3 us (95%)
  local copies, waits for them, and re-layouts  2.46 us (5%)
    pallas_call x1, Pallas kernels, local(): pl.pallas_call(functools.partial(halo_kernel, sizes), out_shape=[array((2...  18.1 us
    pallas_call x1, Pallas kernels, local(): pl.pallas_call(functools.partial(post_kernel, sizes), out_shape=array(hea...  13.7 us
    pallas_call x1, Pallas kernels, local(): pl.pallas_call(functools.partial(gather_kernel, sizes), out_shape=coarse,...  11.3 us
    pallas_call x1, Pallas kernels, local(): pl.pallas_call(pre_kernel, out_shape=[array((6, n, rows, lanes), F32), ar...  5.23 us
    unnamed x6, local copies, waits for them, and re-layouts  2.46 us

profile of v3, /device:TPU:0, one launch (start us, length us, event | category | flops | bytes accessed | tf_op | source)
XLA Modules:
  0.0 50.8 jit_solution(157889083685778894)
XLA Ops:
  0.0 0.0 copy-start
  0.0 0.9 %copy-done = f32[16,16,128]{2,1,0:T(8,128)S(1)} copy-done((f32[16,16,128]{2,1,0:T(8,128)S(1)}, f32[16,16,128]{2,1,0:T(8,128)}, u32[]{:S(2)}) %copy-start) | copy-done | bytes 131096
  0.9 0.0 copy-start.1
  0.9 0.9 %copy-done.1 = s32[16,16,128]{2,1,0:T(8,128)S(1)} copy-done((s32[16,16,128]{2,1,0:T(8,128)S(1)}, s32[16,16,128]{2,1,0:T(8,128)}, u32[]{:S(2)}) %copy-start.1) | copy-done | bytes 131096
  1.8 0.0 copy-start.2
  1.8 0.7 %copy-done.2 = f32[3]{0:T(128)S(1)} copy-done((f32[3]{0:T(128)S(1)}, f32[3]{0:T(128)}, u32[]{:S(2)}) %copy-start.2) | copy-done | bytes 36
  2.5 18.1 %shard_map.37 = (f32[2,28,32,256]{3,2,1,0:T(8,128)S(1)}, f32[2,4,4,4,8,128]{5,4,3,2,1,0:T(8,128)S(1)}) custom-call(f32[16,16,128]{2,1,0:T(8,128)S(1)} %copy-done, s32[16,16,128]{2,1,0:T(8,128)S(1)} %copy-done.1, f32[3]{0:T(128)S(1)} %copy-done.2), custom_call_target="tpu_custom_call" | custom-call | tf_op jit(solution)/shard_map/pallas_call | solution.py:468
  20.6 5.2 %shard_map.38 = (f32[6,28,32,256]{3,2,1,0:T(8,128)S(1)}, f32[28,32,256]{2,1,0:T(8,128)S(1)}, f32[28,32,256]{2,1,0:T(8,128)S(1)}, f32[4,8,128]{2,1,0:T(8,128)S(1)}) custom-call(f32[2,28,32,256]{3,2,1,0:T(8,128)S(1)} %get-tuple-element.11.ext), custom_call_target="tpu_custom_call" | custom-call | tf_op jit(solution)/shard_map/pallas_call | solution.py:489
  25.8 11.3 %shard_map.39.full_right = f32[2,4,4,4,8,128]{5,4,3,2,1,0:T(8,128)S(1)} custom-call(f32[4,8,128]{2,1,0:T(8,128)S(1)} %get-tuple-element.15.block), custom_call_target="tpu_custom_call" | custom-call | tf_op jit(solution)/shard_map/pallas_call | solution.py:502
  37.1 13.7 %shard_map.40 = f32[16,16,128]{2,1,0:T(8,128)} custom-call(f32[6,28,32,256]{3,2,1,0:T(8,128)S(1)} %get-tuple-element.12.faces, f32[28,32,256]{2,1,0:T(8,128)S(1)} %get-tuple-element.13.over, f32[28,32,256]{2,1,0:T(8,128)S(1)} %get-tuple-element.14.start, f32[2,4,4,4,8,128]{5,4,3,2,1,0:T(8,128)S(1)} %shard_map.39.full_right, ...), custom_call_target="tpu_custom_call" | custom-call | tf_op jit(solution)/shard_map/pallas_call | solution.py:521
Async XLA Ops:
  0.0 0.9 %copy-start = (f32[16,16,128]{2,1,0:T(8,128)S(1)}, f32[16,16,128]{2,1,0:T(8,128)}, u32[]{:S(2)}) copy-start(f32[16,16,128]{2,1,0:T(8,128)} %heat.1) | copy-start | bytes 393220
  0.9 0.9 %copy-start.1 = (s32[16,16,128]{2,1,0:T(8,128)S(1)}, s32[16,16,128]{2,1,0:T(8,128)}, u32[]{:S(2)}) copy-start(s32[16,16,128]{2,1,0:T(8,128)} %material.1) | copy-start | bytes 393220
  1.8 0.7 %copy-start.2 = (f32[3]{0:T(128)S(1)}, f32[3]{0:T(128)}, u32[]{:S(2)}) copy-start(f32[3]{0:T(128)} %table.1) | copy-start | bytes 40

commit v4 on v3

--- a/solution.py
+++ b/solution.py
@@ -246,30 +246,16 @@
 
 
 def halo_kernel(
-    sizes, heat, material, table, ext, full,
-    heat_here, material_here, pack, got, sems_out, sems_in, gather_out, gather_in, sems_load,
+    sizes, inputs, ext, full, pack, got, sems_out, sems_in, gather_out, gather_in
 ):
     nx, ny, nz = sizes
     places = ix, iy, iz = tuple(lax.axis_index(axis) for axis in ("gx", "gy", "gz"))
-    bx, by, bz = heat.shape
-    loads = [
-        pltpu.make_async_copy(heat, heat_here, sems_load.at[0]),
-        pltpu.make_async_copy(material, material_here, sems_load.at[1]),
-    ]
-    for load in loads:
-        load.start()
+    bx, by, bz = inputs.shape[1:]
     ext[...] = jnp.zeros(ext.shape, F32)
     got[...] = jnp.zeros(got.shape, F32)
     groups = partner_groups(sizes, places)
     greet(groups)
-    for load in loads:
-        load.wait()
-    own = (pl.ds(HX, bx), pl.ds(HY, by), pl.ds(0, bz))
-    ext[(0, *own)] = heat_here[...]
-    cond = jnp.zeros((bx, by, bz), F32)
-    for which in range(MATERIALS):
-        cond = cond + jnp.where(material_here[...] == which, table[which], 0.0)
-    ext[(1, *own)] = cond
+    ext[:, pl.ds(HX, bx), pl.ds(HY, by), pl.ds(0, bz)] = inputs[...]
     lane = lax.broadcasted_iota(jnp.int32, (by, bz), 1)
     for part in range(2):
         low = jnp.zeros((by, bz), F32)
@@ -316,20 +302,22 @@
         return ext.at[:, pl.ds(start, HX)]
 
     middle = pl.ds(HY, by)
+    full[ix, iz, iy] = pack_block(inputs[1])
+    stages = gather_stages(places, groups, full, gather_out, gather_in)
     await_greetings(groups)
+    start_stage(stages[0])
     sent = [
         send(4, 4, pack.at[0], got.at[1, :, middle], pack.at[1], got.at[0, :, middle]),
         send(2, 2, rows(HY), rows(HY + by), rows(by), rows(0)),
     ]
-    full[ix, iz, iy] = pack_block(cond)
-    stages = gather_stages(places, groups, full, gather_out, gather_in)
-    start_stage(stages[0])
     receive(sent[0])
 
     def edges(start):
         return got.at[:, :, pl.ds(start, HY)]
 
     sent.append(send(2, 6, edges(HY), edges(HY + by), edges(by), edges(0)))
+    end_stage(stages[0])
+    start_stage(stages[1])
     receive(sent[2])
     lane = lax.broadcasted_iota(jnp.int32, (ext.shape[2], bz), 1)
     for part in range(2):
@@ -338,8 +326,6 @@
             v = jnp.where(lane < HZ, pltpu.roll(right, (bz - HZ * x) % bz, 1), 0.0)
             v = jnp.where(lane >= bz - HZ, pltpu.roll(left, (2 * bz - HZ * (x + 1)) % bz, 1), v)
             ext[part, HX + x, :, pl.ds(bz, bz)] = v
-    end_stage(stages[0])
-    start_stage(stages[1])
     receive(sent[1])
     sent.append(send(0, 0, planes(HX), planes(HX + bx), planes(bx), planes(0)))
     end_stage(stages[1])
@@ -458,33 +444,31 @@
     bx, by, bz = heat.shape
     n, rows, lanes = bx + 2 * HX, by + 2 * HY, 2 * bz
     vmem = pl.BlockSpec(memory_space=pltpu.VMEM)
-    smem = pl.BlockSpec(memory_space=pltpu.SMEM)
     limit = 30 * 1024 * 1024
     array = jax.ShapeDtypeStruct
-    hbm = pl.BlockSpec(memory_space=pltpu.HBM)
+    cond = jnp.zeros(heat.shape, F32)
+    for which in range(MATERIALS):
+        cond = cond + jnp.where(material == which, table[which], 0.0)
     count = nx + ny + nz - 3
     coarse = array((nx, nz, ny, bx // 4, by // 2, bz), F32)
     dma = pltpu.SemaphoreType.DMA
     ext, full_cond = pl.pallas_call(
         functools.partial(halo_kernel, sizes),
         out_shape=[array((2, n, rows, lanes), F32), coarse],
-        in_specs=[hbm, hbm, smem],
+        in_specs=[vmem],
         out_specs=[vmem, vmem],
         scratch_shapes=[
-            pltpu.VMEM(heat.shape, F32),
-            pltpu.VMEM(heat.shape, jnp.int32),
             pltpu.VMEM((2, 2, by, bz), F32),
             pltpu.VMEM((2, 2, rows, bz), F32),
             dma((8,)),
             dma((8,)),
             dma((count,)),
             dma((count,)),
-            dma((2,)),
         ],
         compiler_params=pltpu.CompilerParams(
             collective_id=0, has_side_effects=True, vmem_limit_bytes=limit
         ),
-    )(heat, material, table)
+    )(jnp.stack([heat, cond]))
     fine = pltpu.VMEM((n, rows, lanes), F32)
     faces, over, start, packed = pl.pallas_call(
         pre_kernel,

time: 50.9 us -> 50.4 us (level)
  other arithmetic: 0 us -> 3.75 us
  Pallas kernels: 48.3 us -> 45 us
  local copies, waits for them, and re-layouts: 2.46 us -> 1.41 us
    another operation x0 -> x2, other arithmetic: none -> 3.75 us  [local(): jnp.stack([heat, cond])]
    pallas_call x1, Pallas kernels: 18.1 us -> 14.5 us  [local(): pl.pallas_call(functools.partial(halo_kernel, sizes), out_shape=[array((2...]
    unnamed x6 -> x0, local copies, waits for them, and re-layouts: 2.46 us -> none
    slice x0 -> x1, local copies, waits for them, and re-layouts: none -> 1.41 us  [local(): cond = cond + jnp.where(material == which, table[which], 0.0)]
    pallas_call x1, Pallas kernels: 11.3 us -> 11.9 us  [local(): pl.pallas_call(functools.partial(gather_kernel, sizes), out_shape=coarse,...]
where the time goes in v4:
time: 50.4 us; the launch traced here: 50.2 us
  Pallas kernels  45 us (89%)
  other arithmetic  3.75 us (7%)
  local copies, waits for them, and re-layouts  1.41 us (3%)
    pallas_call x1, Pallas kernels, local(): pl.pallas_call(functools.partial(halo_kernel, sizes), out_shape=[array((2...  14.5 us
    pallas_call x1, Pallas kernels, local(): pl.pallas_call(functools.partial(post_kernel, sizes), out_shape=array(hea...  13.6 us
    pallas_call x1, Pallas kernels, local(): pl.pallas_call(functools.partial(gather_kernel, sizes), out_shape=coarse,...  11.9 us
    pallas_call x1, Pallas kernels, local(): pl.pallas_call(pre_kernel, out_shape=[array((6, n, rows, lanes), F32), ar...  5 us
    another operation x2, other arithmetic, local(): jnp.stack([heat, cond])  3.75 us
    slice x1, local copies, waits for them, and re-layouts, local(): cond = cond + jnp.where(material == which, table[which], 0.0)  1.41 us

profile of v4, /device:TPU:0, one launch (start us, length us, event | category | flops | bytes accessed | tf_op | source)
XLA Modules:
  0.0 50.2 jit_solution(17488304294905592387)
XLA Ops:
  0.0 1.4 %fusion = (f32[1]{0:T(128)}, f32[1]{0:T(128)}, f32[1]{0:T(128)}) fusion(f32[3]{0:T(128)} %param.5), kind=kLoop, calls=%fused_computation.2 | loop fusion | bytes 24 | tf_op jit(solution)/shard_map/slice | solution.py:451
  1.4 2.8 %add_bitcast_fusion = f32[1,16,16,128]{3,2,1,0:T(8,128)S(1)} fusion(s32[16,16,128]{2,1,0:T(8,128)} %param.4, f32[]{:T(128)} %bitcast.3, f32[]{:T(128)} %bitcast.2, f32[]{:T(128)} %bitcast.1), kind=kLoop, calls=%fused_computation.1 | loop fusion | flops 262144 | bytes 262156 | tf_op jit(solution)/shard_map/stack | solution.py:471
  4.2 0.9 %pad_maximum_fusion.inputs = f32[2,16,16,128]{3,2,1,0:T(8,128)S(1)} fusion(f32[1,16,16,128]{3,2,1,0:T(8,128)S(1)} %add_bitcast_fusion, f32[1,16,16,128]{3,2,1,0:T(8,128)} %bitcast.6), kind=kLoop, calls=%fused_computation | loop fusion | flops 65536 | bytes 524288 | tf_op jit(solution)/shard_map/stack | solution.py:471
  5.2 14.5 %shard_map.37 = (f32[2,28,32,256]{3,2,1,0:T(8,128)S(1)}, f32[2,4,4,4,8,128]{5,4,3,2,1,0:T(8,128)S(1)}) custom-call(f32[2,16,16,128]{3,2,1,0:T(8,128)S(1)} %pad_maximum_fusion.inputs), custom_call_target="tpu_custom_call" | custom-call | tf_op jit(solution)/shard_map/pallas_call | solution.py:455
  19.7 5.0 %shard_map.38 = (f32[6,28,32,256]{3,2,1,0:T(8,128)S(1)}, f32[28,32,256]{2,1,0:T(8,128)S(1)}, f32[28,32,256]{2,1,0:T(8,128)S(1)}, f32[4,8,128]{2,1,0:T(8,128)S(1)}) custom-call(f32[2,28,32,256]{3,2,1,0:T(8,128)S(1)} %get-tuple-element.11.ext), custom_call_target="tpu_custom_call" | custom-call | tf_op jit(solution)/shard_map/pallas_call | solution.py:473
  24.7 11.9 %shard_map.39.full_right = f32[2,4,4,4,8,128]{5,4,3,2,1,0:T(8,128)S(1)} custom-call(f32[4,8,128]{2,1,0:T(8,128)S(1)} %get-tuple-element.15.block), custom_call_target="tpu_custom_call" | custom-call | tf_op jit(solution)/shard_map/pallas_call | solution.py:486
  36.6 13.6 %shard_map.40 = f32[16,16,128]{2,1,0:T(8,128)} custom-call(f32[6,28,32,256]{3,2,1,0:T(8,128)S(1)} %get-tuple-element.12.faces, f32[28,32,256]{2,1,0:T(8,128)S(1)} %get-tuple-element.13.over, f32[28,32,256]{2,1,0:T(8,128)S(1)} %get-tuple-element.14.start, f32[2,4,4,4,8,128]{5,4,3,2,1,0:T(8,128)S(1)} %shard_map.39.full_right, ...), custom_call_target="tpu_custom_call" | custom-call | tf_op jit(solution)/shard_map/pallas_call | solution.py:505

commit v5 on v4

--- a/solution.py
+++ b/solution.py
@@ -246,16 +246,22 @@
 
 
 def halo_kernel(
-    sizes, inputs, ext, full, pack, got, sems_out, sems_in, gather_out, gather_in
+    sizes, heat, material, table, ext, full,
+    pack, got, sems_out, sems_in, gather_out, gather_in,
 ):
     nx, ny, nz = sizes
     places = ix, iy, iz = tuple(lax.axis_index(axis) for axis in ("gx", "gy", "gz"))
-    bx, by, bz = inputs.shape[1:]
+    bx, by, bz = heat.shape
     ext[...] = jnp.zeros(ext.shape, F32)
     got[...] = jnp.zeros(got.shape, F32)
     groups = partner_groups(sizes, places)
     greet(groups)
-    ext[:, pl.ds(HX, bx), pl.ds(HY, by), pl.ds(0, bz)] = inputs[...]
+    own = (pl.ds(HX, bx), pl.ds(HY, by), pl.ds(0, bz))
+    ext[(0, *own)] = heat[...]
+    cond = jnp.zeros((bx, by, bz), F32)
+    for which in range(MATERIALS):
+        cond = cond + jnp.where(material[...] == which, table[which], 0.0)
+    ext[(1, *own)] = cond
     lane = lax.broadcasted_iota(jnp.int32, (by, bz), 1)
     for part in range(2):
         low = jnp.zeros((by, bz), F32)
@@ -302,7 +308,7 @@
         return ext.at[:, pl.ds(start, HX)]
 
     middle = pl.ds(HY, by)
-    full[ix, iz, iy] = pack_block(inputs[1])
+    full[ix, iz, iy] = pack_block(cond)
     stages = gather_stages(places, groups, full, gather_out, gather_in)
     await_greetings(groups)
     start_stage(stages[0])
@@ -444,18 +450,16 @@
     bx, by, bz = heat.shape
     n, rows, lanes = bx + 2 * HX, by + 2 * HY, 2 * bz
     vmem = pl.BlockSpec(memory_space=pltpu.VMEM)
+    smem = pl.BlockSpec(memory_space=pltpu.SMEM)
     limit = 30 * 1024 * 1024
     array = jax.ShapeDtypeStruct
-    cond = jnp.zeros(heat.shape, F32)
-    for which in range(MATERIALS):
-        cond = cond + jnp.where(material == which, table[which], 0.0)
     count = nx + ny + nz - 3
     coarse = array((nx, nz, ny, bx // 4, by // 2, bz), F32)
     dma = pltpu.SemaphoreType.DMA
     ext, full_cond = pl.pallas_call(
         functools.partial(halo_kernel, sizes),
         out_shape=[array((2, n, rows, lanes), F32), coarse],
-        in_specs=[vmem],
+        in_specs=[vmem, vmem, smem],
         out_specs=[vmem, vmem],
         scratch_shapes=[
             pltpu.VMEM((2, 2, by, bz), F32),
@@ -468,7 +472,7 @@
         compiler_params=pltpu.CompilerParams(
             collective_id=0, has_side_effects=True, vmem_limit_bytes=limit
         ),
-    )(jnp.stack([heat, cond]))
+    )(heat, material, table)
     fine = pltpu.VMEM((n, rows, lanes), F32)
     faces, over, start, packed = pl.pallas_call(
         pre_kernel,

time: 50.4 us -> 48.6 us (0.964)
  other arithmetic: 3.75 us -> 0 us
  local copies, waits for them, and re-layouts: 1.41 us -> 2.46 us
  Pallas kernels: 45 us -> 45.9 us
    another operation x2 -> x0, other arithmetic: 3.75 us -> none  [local(): jnp.stack([heat, cond])]
    unnamed x0 -> x6, local copies, waits for them, and re-layouts: none -> 2.46 us
    slice x1 -> x0, local copies, waits for them, and re-layouts: 1.41 us -> none  [local(): cond = cond + jnp.where(material == which, table[which], 0.0)]
    pallas_call x1, Pallas kernels: 14.5 us -> 15 us  [local(): pl.pallas_call(functools.partial(halo_kernel, sizes), out_shape=[array((2...]
where the time goes in v5:
time: 48.6 us; the launch traced here: 48.4 us
  Pallas kernels  45.9 us (94%)
  local copies, waits for them, and re-layouts  2.46 us (5%)
    pallas_call x1, Pallas kernels, local(): pl.pallas_call(functools.partial(halo_kernel, sizes), out_shape=[array((2...  15 us
    pallas_call x1, Pallas kernels, local(): pl.pallas_call(functools.partial(post_kernel, sizes), out_shape=array(hea...  13.7 us
    pallas_call x1, Pallas kernels, local(): pl.pallas_call(functools.partial(gather_kernel, sizes), out_shape=coarse,...  11.9 us
    pallas_call x1, Pallas kernels, local(): pl.pallas_call(pre_kernel, out_shape=[array((6, n, rows, lanes), F32), ar...  5.23 us
    unnamed x6, local copies, waits for them, and re-layouts  2.46 us

profile of v5, /device:TPU:0, one launch (start us, length us, event | category | flops | bytes accessed | tf_op | source)
XLA Modules:
  0.0 48.4 jit_solution(472233303315319435)
XLA Ops:
  0.0 0.0 copy-start
  0.0 0.9 %copy-done = f32[16,16,128]{2,1,0:T(8,128)S(1)} copy-done((f32[16,16,128]{2,1,0:T(8,128)S(1)}, f32[16,16,128]{2,1,0:T(8,128)}, u32[]{:S(2)}) %copy-start) | copy-done | bytes 131096
  0.9 0.0 copy-start.1
  0.9 0.9 %copy-done.1 = s32[16,16,128]{2,1,0:T(8,128)S(1)} copy-done((s32[16,16,128]{2,1,0:T(8,128)S(1)}, s32[16,16,128]{2,1,0:T(8,128)}, u32[]{:S(2)}) %copy-start.1) | copy-done | bytes 131096
  1.8 0.0 copy-start.2
  1.8 0.7 %copy-done.2 = f32[3]{0:T(128)S(1)} copy-done((f32[3]{0:T(128)S(1)}, f32[3]{0:T(128)}, u32[]{:S(2)}) %copy-start.2) | copy-done | bytes 36
  2.5 15.0 %shard_map.37 = (f32[2,28,32,256]{3,2,1,0:T(8,128)S(1)}, f32[2,4,4,4,8,128]{5,4,3,2,1,0:T(8,128)S(1)}) custom-call(f32[16,16,128]{2,1,0:T(8,128)S(1)} %copy-done, s32[16,16,128]{2,1,0:T(8,128)S(1)} %copy-done.1, f32[3]{0:T(128)S(1)} %copy-done.2), custom_call_target="tpu_custom_call" | custom-call | tf_op jit(solution)/shard_map/pallas_call | solution.py:459
  17.5 5.2 %shard_map.38 = (f32[6,28,32,256]{3,2,1,0:T(8,128)S(1)}, f32[28,32,256]{2,1,0:T(8,128)S(1)}, f32[28,32,256]{2,1,0:T(8,128)S(1)}, f32[4,8,128]{2,1,0:T(8,128)S(1)}) custom-call(f32[2,28,32,256]{3,2,1,0:T(8,128)S(1)} %get-tuple-element.11.ext), custom_call_target="tpu_custom_call" | custom-call | tf_op jit(solution)/shard_map/pallas_call | solution.py:477
  22.7 11.9 %shard_map.39.full_right = f32[2,4,4,4,8,128]{5,4,3,2,1,0:T(8,128)S(1)} custom-call(f32[4,8,128]{2,1,0:T(8,128)S(1)} %get-tuple-element.15.block), custom_call_target="tpu_custom_call" | custom-call | tf_op jit(solution)/shard_map/pallas_call | solution.py:490
  34.7 13.7 %shard_map.40 = f32[16,16,128]{2,1,0:T(8,128)} custom-call(f32[6,28,32,256]{3,2,1,0:T(8,128)S(1)} %get-tuple-element.12.faces, f32[28,32,256]{2,1,0:T(8,128)S(1)} %get-tuple-element.13.over, f32[28,32,256]{2,1,0:T(8,128)S(1)} %get-tuple-element.14.start, f32[2,4,4,4,8,128]{5,4,3,2,1,0:T(8,128)S(1)} %shard_map.39.full_right, ...), custom_call_target="tpu_custom_call" | custom-call | tf_op jit(solution)/shard_map/pallas_call | solution.py:509
Async XLA Ops:
  0.0 0.9 %copy-start = (f32[16,16,128]{2,1,0:T(8,128)S(1)}, f32[16,16,128]{2,1,0:T(8,128)}, u32[]{:S(2)}) copy-start(f32[16,16,128]{2,1,0:T(8,128)} %heat.1) | copy-start | bytes 393220
  0.9 0.9 %copy-start.1 = (s32[16,16,128]{2,1,0:T(8,128)S(1)}, s32[16,16,128]{2,1,0:T(8,128)}, u32[]{:S(2)}) copy-start(s32[16,16,128]{2,1,0:T(8,128)} %material.1) | copy-start | bytes 393220
  1.8 0.7 %copy-start.2 = (f32[3]{0:T(128)S(1)}, f32[3]{0:T(128)}, u32[]{:S(2)}) copy-start(f32[3]{0:T(128)} %table.1) | copy-start | bytes 40

commit v6 on v5

--- a/solution.py
+++ b/solution.py
@@ -215,12 +215,13 @@
 
 def gather_stages(places, groups, full, sems_out, sems_in):
     ix, iy, iz = places
-    slot = 0
-    stages = []
-    for group, source in zip(groups, (full.at[ix, iz, iy], full.at[ix, iz], full.at[ix])):
-        stage = []
+    slots = iter(range(sems_out.shape[0]))
+
+    def copies(group, source):
+        made = []
         for axis, other in group:
-            stage.append(
+            slot = next(slots)
+            made.append(
                 pltpu.make_async_remote_copy(
                     src_ref=source,
                     dst_ref=source,
@@ -230,9 +231,34 @@
                     device_id_type=MESH,
                 )
             )
-            slot += 1
-        stages.append(stage)
-    return stages
+        return made
+
+    along_y = copies(groups[0], full.at[ix, iz, iy])
+    along_z = copies(groups[1], full.at[ix, iz])
+    count = full.shape[1]
+    columns = [
+        copies(groups[2], full.at[ix, lax.rem(iz + count - off, count)]) for off in range(count)
+    ]
+    return along_y, along_z, columns
+
+
+def middle_stage(stages):
+    end_stage(stages[0])
+    start_stage(stages[1])
+    start_stage(stages[2][0])
+
+
+def last_stage(stages):
+    for copy, column in zip(stages[1], stages[2][1:]):
+        copy.wait_recv()
+        start_stage(column)
+
+
+def end_gather(stages):
+    for column in stages[2]:
+        end_stage(column)
+    for copy in sum(stages[2], stages[0] + stages[1]):
+        copy.wait_send()
 
 
 def start_stage(stage):
@@ -322,8 +348,7 @@
         return got.at[:, :, pl.ds(start, HY)]
 
     sent.append(send(2, 6, edges(HY), edges(HY + by), edges(by), edges(0)))
-    end_stage(stages[0])
-    start_stage(stages[1])
+    middle_stage(stages)
     receive(sent[2])
     lane = lax.broadcasted_iota(jnp.int32, (ext.shape[2], bz), 1)
     for part in range(2):
@@ -334,16 +359,12 @@
             ext[part, HX + x, :, pl.ds(bz, bz)] = v
     receive(sent[1])
     sent.append(send(0, 0, planes(HX), planes(HX + bx), planes(bx), planes(0)))
-    end_stage(stages[1])
-    start_stage(stages[2])
+    last_stage(stages)
     receive(sent[3])
-    end_stage(stages[2])
     for copies in sent:
         for there, copy in copies:
             pl.when(there)(copy.wait_send)
-    for stage in stages:
-        for copy in stage:
-            copy.wait_send()
+    end_gather(stages)
 
 
 def pre_kernel(ext, faces, over, field, packed, diagonal, step, temp):
@@ -371,12 +392,10 @@
     full[ix, iz, iy] = block[...]
     await_greetings(groups)
     stages = gather_stages(places, groups, full, sems_out, sems_in)
-    for stage in stages:
-        start_stage(stage)
-        end_stage(stage)
-    for stage in stages:
-        for copy in stage:
-            copy.wait_send()
+    start_stage(stages[0])
+    middle_stage(stages)
+    last_stage(stages)
+    end_gather(stages)
 
 
 def post_kernel(sizes, faces, over, start, full_right, full_cond, out, *scratch):
@@ -453,7 +472,7 @@
     smem = pl.BlockSpec(memory_space=pltpu.SMEM)
     limit = 30 * 1024 * 1024
     array = jax.ShapeDtypeStruct
-    count = nx + ny + nz - 3
+    count = ny - 1 + nz - 1 + (nx - 1) * nz
     coarse = array((nx, nz, ny, bx // 4, by // 2, bz), F32)
     dma = pltpu.SemaphoreType.DMA
     ext, full_cond = pl.pallas_call(

time: 48.6 us -> 48.2 us (level)
  no operation moved by 1% of the time
where the time goes in v6:
time: 48.2 us; the launch traced here: 48.1 us
  Pallas kernels  45.6 us (95%)
  local copies, waits for them, and re-layouts  2.46 us (5%)
    pallas_call x1, Pallas kernels, local(): pl.pallas_call(functools.partial(halo_kernel, sizes), out_shape=[array((2...  14.9 us
    pallas_call x1, Pallas kernels, local(): pl.pallas_call(functools.partial(post_kernel, sizes), out_shape=array(hea...  13.7 us
    pallas_call x1, Pallas kernels, local(): pl.pallas_call(functools.partial(gather_kernel, sizes), out_shape=coarse,...  11.7 us
    pallas_call x1, Pallas kernels, local(): pl.pallas_call(pre_kernel, out_shape=[array((6, n, rows, lanes), F32), ar...  5.23 us
    unnamed x6, local copies, waits for them, and re-layouts  2.46 us

profile of v6, /device:TPU:0, one launch (start us, length us, event | category | flops | bytes accessed | tf_op | source)
XLA Modules:
  0.0 48.1 jit_solution(8445835050606200530)
XLA Ops:
  0.0 0.0 copy-start
  0.0 0.9 %copy-done = f32[16,16,128]{2,1,0:T(8,128)S(1)} copy-done((f32[16,16,128]{2,1,0:T(8,128)S(1)}, f32[16,16,128]{2,1,0:T(8,128)}, u32[]{:S(2)}) %copy-start) | copy-done | bytes 131096
  0.9 0.0 copy-start.1
  0.9 0.9 %copy-done.1 = s32[16,16,128]{2,1,0:T(8,128)S(1)} copy-done((s32[16,16,128]{2,1,0:T(8,128)S(1)}, s32[16,16,128]{2,1,0:T(8,128)}, u32[]{:S(2)}) %copy-start.1) | copy-done | bytes 131096
  1.8 0.0 copy-start.2
  1.8 0.7 %copy-done.2 = f32[3]{0:T(128)S(1)} copy-done((f32[3]{0:T(128)S(1)}, f32[3]{0:T(128)}, u32[]{:S(2)}) %copy-start.2) | copy-done | bytes 36
  2.5 14.9 %shard_map.37 = (f32[2,28,32,256]{3,2,1,0:T(8,128)S(1)}, f32[2,4,4,4,8,128]{5,4,3,2,1,0:T(8,128)S(1)}) custom-call(f32[16,16,128]{2,1,0:T(8,128)S(1)} %copy-done, s32[16,16,128]{2,1,0:T(8,128)S(1)} %copy-done.1, f32[3]{0:T(128)S(1)} %copy-done.2), custom_call_target="tpu_custom_call" | custom-call | tf_op jit(solution)/shard_map/pallas_call | solution.py:478
  17.4 5.2 %shard_map.38 = (f32[6,28,32,256]{3,2,1,0:T(8,128)S(1)}, f32[28,32,256]{2,1,0:T(8,128)S(1)}, f32[28,32,256]{2,1,0:T(8,128)S(1)}, f32[4,8,128]{2,1,0:T(8,128)S(1)}) custom-call(f32[2,28,32,256]{3,2,1,0:T(8,128)S(1)} %get-tuple-element.11.ext), custom_call_target="tpu_custom_call" | custom-call | tf_op jit(solution)/shard_map/pallas_call | solution.py:496
  22.6 11.7 %shard_map.39.full_right = f32[2,4,4,4,8,128]{5,4,3,2,1,0:T(8,128)S(1)} custom-call(f32[4,8,128]{2,1,0:T(8,128)S(1)} %get-tuple-element.15.block), custom_call_target="tpu_custom_call" | custom-call | tf_op jit(solution)/shard_map/pallas_call | solution.py:509
  34.4 13.7 %shard_map.40 = f32[16,16,128]{2,1,0:T(8,128)} custom-call(f32[6,28,32,256]{3,2,1,0:T(8,128)S(1)} %get-tuple-element.12.faces, f32[28,32,256]{2,1,0:T(8,128)S(1)} %get-tuple-element.13.over, f32[28,32,256]{2,1,0:T(8,128)S(1)} %get-tuple-element.14.start, f32[2,4,4,4,8,128]{5,4,3,2,1,0:T(8,128)S(1)} %shard_map.39.full_right, ...), custom_call_target="tpu_custom_call" | custom-call | tf_op jit(solution)/shard_map/pallas_call | solution.py:528
Async XLA Ops:
  0.0 0.9 %copy-start = (f32[16,16,128]{2,1,0:T(8,128)S(1)}, f32[16,16,128]{2,1,0:T(8,128)}, u32[]{:S(2)}) copy-start(f32[16,16,128]{2,1,0:T(8,128)} %heat.1) | copy-start | bytes 393220
  0.9 0.9 %copy-start.1 = (s32[16,16,128]{2,1,0:T(8,128)S(1)}, s32[16,16,128]{2,1,0:T(8,128)}, u32[]{:S(2)}) copy-start(s32[16,16,128]{2,1,0:T(8,128)} %material.1) | copy-start | bytes 393220
  1.8 0.7 %copy-start.2 = (f32[3]{0:T(128)S(1)}, f32[3]{0:T(128)}, u32[]{:S(2)}) copy-start(f32[3]{0:T(128)} %table.1) | copy-start | bytes 40

commit v7 on v6

--- a/solution.py
+++ b/solution.py
@@ -89,7 +89,7 @@
 
 def residuals(lo, hi, field, coefs, use):
     faces, over = coefs[:2]
-    group = min(hi - lo, 8 if field.shape[1] <= 16 else 4)
+    group = min(hi - lo, 4 if (hi - lo) % 8 else 8)
 
     def body(turn, carry):
         start = lo + turn * group

time: 48.2 us -> 46.8 us (0.971)
  Pallas kernels: 45.6 us -> 44.1 us
    pallas_call x1, Pallas kernels: 13.7 us -> 12.8 us  [local(): pl.pallas_call(functools.partial(post_kernel, sizes), out_shape=array(hea...]
    pallas_call x1, Pallas kernels: 5.23 us -> 4.7 us  [local(): pl.pallas_call(pre_kernel, out_shape=[array((6, n, rows, lanes), F32), ar...]
where the time goes in v7:
time: 46.8 us; the launch traced here: 46.6 us
  Pallas kernels  44.1 us (94%)
  local copies, waits for them, and re-layouts  2.46 us (5%)
    pallas_call x1, Pallas kernels, local(): pl.pallas_call(functools.partial(halo_kernel, sizes), out_shape=[array((2...  14.9 us
    pallas_call x1, Pallas kernels, local(): pl.pallas_call(functools.partial(post_kernel, sizes), out_shape=array(hea...  12.8 us
    pallas_call x1, Pallas kernels, local(): pl.pallas_call(functools.partial(gather_kernel, sizes), out_shape=coarse,...  11.7 us
    pallas_call x1, Pallas kernels, local(): pl.pallas_call(pre_kernel, out_shape=[array((6, n, rows, lanes), F32), ar...  4.7 us
    unnamed x6, local copies, waits for them, and re-layouts  2.46 us

profile of v7, /device:TPU:0, one launch (start us, length us, event | category | flops | bytes accessed | tf_op | source)
XLA Modules:
  0.0 46.6 jit_solution(13851709944547589682)
XLA Ops:
  0.0 0.0 copy-start
  0.0 0.9 %copy-done = f32[16,16,128]{2,1,0:T(8,128)S(1)} copy-done((f32[16,16,128]{2,1,0:T(8,128)S(1)}, f32[16,16,128]{2,1,0:T(8,128)}, u32[]{:S(2)}) %copy-start) | copy-done | bytes 131096
  0.9 0.0 copy-start.1
  0.9 0.9 %copy-done.1 = s32[16,16,128]{2,1,0:T(8,128)S(1)} copy-done((s32[16,16,128]{2,1,0:T(8,128)S(1)}, s32[16,16,128]{2,1,0:T(8,128)}, u32[]{:S(2)}) %copy-start.1) | copy-done | bytes 131096
  1.8 0.0 copy-start.2
  1.8 0.7 %copy-done.2 = f32[3]{0:T(128)S(1)} copy-done((f32[3]{0:T(128)S(1)}, f32[3]{0:T(128)}, u32[]{:S(2)}) %copy-start.2) | copy-done | bytes 36
  2.5 14.9 %shard_map.37 = (f32[2,28,32,256]{3,2,1,0:T(8,128)S(1)}, f32[2,4,4,4,8,128]{5,4,3,2,1,0:T(8,128)S(1)}) custom-call(f32[16,16,128]{2,1,0:T(8,128)S(1)} %copy-done, s32[16,16,128]{2,1,0:T(8,128)S(1)} %copy-done.1, f32[3]{0:T(128)S(1)} %copy-done.2), custom_call_target="tpu_custom_call" | custom-call | tf_op jit(solution)/shard_map/pallas_call | solution.py:478
  17.4 4.7 %shard_map.38 = (f32[6,28,32,256]{3,2,1,0:T(8,128)S(1)}, f32[28,32,256]{2,1,0:T(8,128)S(1)}, f32[28,32,256]{2,1,0:T(8,128)S(1)}, f32[4,8,128]{2,1,0:T(8,128)S(1)}) custom-call(f32[2,28,32,256]{3,2,1,0:T(8,128)S(1)} %get-tuple-element.11.ext), custom_call_target="tpu_custom_call" | custom-call | tf_op jit(solution)/shard_map/pallas_call | solution.py:496
  22.1 11.7 %shard_map.39.full_right = f32[2,4,4,4,8,128]{5,4,3,2,1,0:T(8,128)S(1)} custom-call(f32[4,8,128]{2,1,0:T(8,128)S(1)} %get-tuple-element.15.block), custom_call_target="tpu_custom_call" | custom-call | tf_op jit(solution)/shard_map/pallas_call | solution.py:509
  33.8 12.8 %shard_map.40 = f32[16,16,128]{2,1,0:T(8,128)} custom-call(f32[6,28,32,256]{3,2,1,0:T(8,128)S(1)} %get-tuple-element.12.faces, f32[28,32,256]{2,1,0:T(8,128)S(1)} %get-tuple-element.13.over, f32[28,32,256]{2,1,0:T(8,128)S(1)} %get-tuple-element.14.start, f32[2,4,4,4,8,128]{5,4,3,2,1,0:T(8,128)S(1)} %shard_map.39.full_right, ...), custom_call_target="tpu_custom_call" | custom-call | tf_op jit(solution)/shard_map/pallas_call | solution.py:528
Async XLA Ops:
  0.0 0.9 %copy-start = (f32[16,16,128]{2,1,0:T(8,128)S(1)}, f32[16,16,128]{2,1,0:T(8,128)}, u32[]{:S(2)}) copy-start(f32[16,16,128]{2,1,0:T(8,128)} %heat.1) | copy-start | bytes 393220
  0.9 0.9 %copy-start.1 = (s32[16,16,128]{2,1,0:T(8,128)S(1)}, s32[16,16,128]{2,1,0:T(8,128)}, u32[]{:S(2)}) copy-start(s32[16,16,128]{2,1,0:T(8,128)} %material.1) | copy-start | bytes 393220
  1.8 0.7 %copy-start.2 = (f32[3]{0:T(128)S(1)}, f32[3]{0:T(128)}, u32[]{:S(2)}) copy-start(f32[3]{0:T(128)} %table.1) | copy-start | bytes 40
